TPU v7x, 256 devices: a whole 4x4x8 slice. The times are simulated.
256 devices in a mesh: scan: 128 (over y, z, x), det: 2 (over core).
Axes of the slice: x: 4, y: 4, z: 8, core: 2. Of those that a mesh axis runs over, the one named last changes fastest.
Arguments:
- frames: float32 [256, 512, 512], P('det', 'scan'), may hold values from -6 to 6
- aperture: int32 [256], replicated, may hold values 0 or 1
- upper_pixels: int32 [128, 64], replicated, may hold values from -1 to 255, as said below
- lower_pixels: int32 [128, 64], replicated, may hold values from -1 to 255, as said below
Outputs:
- spectrum: float32 [2, 512, 512], P(None, 'scan', 'det')
- object_wave: float32 [2, 512, 512], P(None, 'det', 'scan')
Inputs may be any that keep to these rules, and one draw needn't show every extreme that they name: `upper_pixels`: each row lists pixels of one frequency block: 1 to 64 pixel numbers, then -1 to the end of the row; some row is full and some row has a single entry. A pixel may appear more than once. `lower_pixels`: as for upper_pixels.
All inputs are finite; a program needn't handle non-finite values.
Results may differ from a plain program's by a relative error of at most 0.0001.
Values sent between devices are 32-bit elements; how exact they have to be, the bound alone decides.
A program may use at most 192 MiB of HBM per device.

v0:
```python
import math

import jax
import jax.numpy as jnp
from jax import lax
from jax.experimental import pallas as pl
from jax.experimental.pallas import tpu as pltpu
from jax.sharding import PartitionSpec as P

MESH = pl.DeviceIdType.MESH
F32 = jnp.float32
BF16 = jnp.bfloat16
UNIT = 2.0 * math.pi / 512
SIN = (-1.0 / 6, 1.0 / 120, -1.0 / 5040, 1.0 / 362880, -1.0 / 39916800)


def cos512(m):
    m = m & 511
    t = (128 - jnp.minimum(m, 512 - m)).astype(F32) * UNIT
    t2 = t * t
    poly = jnp.full_like(t, SIN[-1])
    for coefficient in SIN[-2::-1]:
        poly = poly * t2 + coefficient
    return t + t * (t2 * poly)


def split(a):
    high = a.astype(BF16)
    return high, (a - high.astype(F32)).astype(BF16)


def dot(a, b):
    return jnp.dot(a, b, preferred_element_type=F32)


def dot3(a, b_high, b_low):
    rows = a.shape[0]
    a_high, a_low = split(a)
    both = dot(jnp.concatenate((a_high, a_low), axis=0), b_high)
    return both[:rows] + both[rows:] + dot(a_high, b_low)


def iota(shape, dimension):
    return lax.broadcasted_iota(jnp.int32, shape, dimension)


def kernel(
    frames, aperture, upper, lower,
    spectrum, wave,
    f, ap, up, lo, w_lo, w_hi,
    a, r1, t1, r2, t2, r3, t3, r_pair, turned, pm, r4, q, r5, e_high, e_low,
    load_sem, pair_sem, sem1, sem2, sem3, sem4, send5, recv5,
):
    s = lax.axis_index("scan")
    c = lax.axis_index("det")
    y, z, x = s // 32, (s // 4) % 8, s % 4
    u, v = x * (1 - c) + y * c, y * (1 - c) + x * c
    su, sv = 1 - c + 32 * c, 32 * (1 - c) + c

    loads = [
        pltpu.make_async_copy(upper, up, load_sem.at[0]),
        pltpu.make_async_copy(lower, lo, load_sem.at[1]),
        pltpu.make_async_copy(aperture, ap, load_sem.at[2]),
        pltpu.make_async_copy(frames.at[:, c], f.at[pl.ds(c * 128, 128)], load_sem.at[3]),
    ]
    for load in loads:
        load.start()

    def u_peer(d):
        return s + ((u + d) % 4 - u) * su

    def v_peer(d):
        return s + ((v + d) % 4 - v) * sv

    def z_peer(d):
        return s + ((z + d) % 8 - z) * 4

    barrier = pltpu.get_barrier_semaphore()

    def greet(scan, det):
        pl.semaphore_signal(barrier, inc=1, device_id=(scan, det), device_id_type=MESH)

    greet(s, 1 - c)
    for d in range(1, 4):
        greet(u_peer(d), c)
        greet(v_peer(d), c)
    for d in range(1, 8):
        greet(z_peer(d), c)
    source_core = y // 2
    for i in range(16):
        chip = (i // 4) * 32 + z * 4 + i % 4

        @pl.when(jnp.logical_or(chip != s, source_core != c))
        def _():
            greet(chip, source_core)

    own = jnp.where(source_core == c, 1, 0)
    pl.semaphore_wait(barrier, 30 - own)

    swap = pltpu.make_async_remote_copy(
        src_ref=frames.at[:, 1 - c], dst_ref=f.at[pl.ds(c * 128, 128)],
        send_sem=pair_sem.at[0], recv_sem=pair_sem.at[1], device_id=(s, 1 - c), device_id_type=MESH,
    )
    swap.start()

    for load in loads[:3]:
        load.wait()
    pixel = iota((256, 128), 0)

    def count(j, total):
        plus = jnp.where(up[pl.ds(j, 1), :] == pixel, 1, 0)
        return total + plus - jnp.where(lo[pl.ds(j, 1), :] == pixel, 1, 0)

    counts = lax.fori_loop(0, 64, count, jnp.zeros((256, 128), jnp.int32))
    scaled = counts.astype(F32) * (64**-0.5 / 512)
    w_lo[...] = scaled[:128].T
    w_hi[...] = scaled[128:].T
    inside = ap[...].astype(F32)
    tiles = []
    for i in range(16):
        start = (i // 4) * su + (i % 4) * sv
        rows = pl.ds(start, 8, stride=4)
        tiles.append(jnp.concatenate((w_lo[rows, :], w_hi[rows, :]), axis=1))
    weight = (jnp.concatenate(tiles, axis=0) * inside).astype(BF16)

    loads[3].wait()
    swap.wait_recv()
    flat = f.reshape(2048, 128)
    for i in range(4):
        part = jnp.concatenate([flat[pl.ds(4 * j + i, 256, stride=8), :] for j in range(2)], axis=1)
        high, low = split(part)
        total = dot(weight, high) + dot(weight, low)
        a[:, :, i] = total.reshape(4, 4, 8, 256)

    first = []
    for d in range(1, 4):
        first.append(pltpu.make_async_remote_copy(
            src_ref=a.at[(u + d) % 4], dst_ref=r1.at[d - 1], send_sem=sem1.at[0, d - 1], recv_sem=sem1.at[1, d - 1],
            device_id=(u_peer(d), c), device_id_type=MESH,
        ))
    for copy in first:
        copy.start()

    frequency = iota((256, 512), 1)
    wide = frequency % 256 + 256 * c
    table = cos512(wide * iota((256, 512), 0) - 128 * (frequency // 256))
    table_high, table_low = split(table)
    e_high[...] = table_high
    e_low[...] = table_low

    row, column = iota((64, 128), 0), iota((64, 128), 1)
    rho = row % 8
    place = 4 * (((u - column // 32) & 3) * su + v * sv + 4 * z) + (column // 8) % 4
    same = (row // 8) == (column % 8)
    lefts = []
    for d in range(4):
        block = u * su + ((v + d) % 4) * sv + 4 * (row // 8)
        left = cos512((4 * block + rho % 4) * place + 128 * (rho // 4))
        lefts.append(split(jnp.where(same, left, 0.0)))

    for copy in first:
        copy.wait_recv()

    second = []
    for d in (1, 2, 3, 0):
        vb = (v + d) % 4
        rows = [a[u, vb].reshape(32, 256)] + [r1[j, vb].reshape(32, 256) for j in range(3)]
        right_high, right_low = split(jnp.concatenate(rows, axis=0))
        left_high, left_low = lefts[d]
        both = dot(jnp.concatenate((left_high, left_low), axis=0), right_high)
        t1[d] = both[:64] + both[64:] + dot(left_high, right_low)
        if d:
            copy = pltpu.make_async_remote_copy(
                src_ref=t1.at[d], dst_ref=r2.at[d - 1], send_sem=sem2.at[0, d - 1], recv_sem=sem2.at[1, d - 1],
                device_id=(v_peer(d), c), device_id_type=MESH,
            )
            copy.start()
            second.append(copy)
    for copy in second:
        copy.wait_recv()
    t2[...] = (t1[0] + r2[0] + r2[1] + r2[2]).reshape(8, 8, 256)

    third = []
    for d in range(1, 8):
        copy = pltpu.make_async_remote_copy(
            src_ref=t2.at[(z + d) % 8], dst_ref=r3.at[d - 1], send_sem=sem3.at[0, d - 1], recv_sem=sem3.at[1, d - 1],
            device_id=(z_peer(d), c), device_id_type=MESH,
        )
        copy.start()
        third.append(copy)
    n = iota((128, 256), 1)
    source = iota((128, 256), 0)
    source_block = (source // 32) * 32 + (source // 8) % 4 + 4 * ((z - source % 8) & 7)
    back_high, back_low = split(cos512(4 * source_block * (n % 128) - 128 * (n // 128)))
    for copy in third:
        copy.wait_recv()
    total = t2[z]
    for d in range(7):
        total = total + r3[d]
    t3[...] = total

    other = pltpu.make_async_remote_copy(
        src_ref=t3, dst_ref=r_pair, send_sem=pair_sem.at[2], recv_sem=pair_sem.at[3],
        device_id=(s, 1 - c), device_id_type=MESH,
    )
    other.start()

    lane = iota((32, 128), 1)
    for half in range(2):
        tile = total[:, half * 128 : (half + 1) * 128]
        turned[...] = jnp.concatenate([tile] * 16, axis=0).T
        packed = jnp.zeros((32, 128), F32)
        for i in range(4):
            packed = jnp.where(lane // 8 == i, turned[pl.ds(i, 32, stride=4), :], packed)
        for i in range(8):
            pm[i, half * 4 : half * 4 + 4, :] = packed[i * 4 : i * 4 + 4]
    fourth = []
    for d in range(1, 8):
        copy = pltpu.make_async_remote_copy(
            src_ref=pm.at[(z + d) % 8], dst_ref=r4.at[d], send_sem=sem4.at[0, d - 1], recv_sem=sem4.at[1, d - 1],
            device_id=(z_peer(d), c), device_id_type=MESH,
        )
        copy.start()
        fourth.append(copy)
    r4[0] = pm[z]
    for copy in fourth:
        copy.wait_recv()

    flat4 = r4.reshape(64, 128)
    me = y * 4 + x
    for i in range(8):
        q[i] = flat4[pl.ds(i, 8, stride=8), :]

    def out_copy(i, core, chip):
        return pltpu.make_async_remote_copy(
            src_ref=q.at[i], dst_ref=r5.at[me], send_sem=send5.at[2 * i + core], recv_sem=recv5.at[me],
            device_id=(chip, core), device_id_type=MESH,
        )

    for i in range(8):
        chip = (2 * c + i // 4) * 32 + z * 4 + i % 4
        for core in range(2):
            mine = jnp.logical_and(chip == s, c == core)

            @pl.when(jnp.logical_not(mine))
            def _():
                out_copy(i, core, chip).start()

            @pl.when(mine)
            def _():
                pltpu.make_async_copy(q.at[i], r5.at[me], recv5.at[me]).start()

    other.wait_recv()
    sums = dot3(jnp.concatenate((total, r_pair[...]), axis=0), e_high[...], e_low[...])
    lane = iota((8, 256), 1)
    sign = (1 - 2 * (lane % 2)).astype(F32)
    near, far = jnp.where(c == 0, 1.0, sign), jnp.where(c == 0, sign, 1.0)
    cosine = near * sums[:8, :256] + far * sums[8:, :256]
    sine = near * sums[:8, 256:] + far * sums[8:, 256:]
    side = jnp.where(iota((8, 256), 0) < 4, -1.0, 1.0)
    result = cosine - side * jnp.concatenate((sine[4:], sine[:4]), axis=0)
    spectrum[0] = result[:4]
    spectrum[1] = result[4:]

    rho = iota((8, 256), 0)
    angle = (rho % 4) * (lane + 256 * c) + 128 * (rho // 4)
    turn_real, turn_imag = cos512(angle), cos512(angle - 128)

    for i in range(16):
        pltpu.make_async_copy(q.at[0], r5.at[i], recv5.at[i]).wait()
    right = r5.reshape(128, 128)[...].T[:32]
    moved = dot3(right, back_high, back_low)
    reals, imags = [], []
    for i in range(4):
        tile = moved[8 * i : 8 * i + 8]
        sine = tile[:, 128:]
        pair = tile[:, :128] + side[:, :128] * jnp.concatenate((sine[4:], sine[:4]), axis=0)
        twice = jnp.concatenate((pair, pair), axis=1)
        reals.append(jnp.sum(twice * turn_real, axis=0, keepdims=True))
        imags.append(jnp.sum(twice * turn_imag, axis=0, keepdims=True))
    wave[0] = jnp.concatenate(reals, axis=0)
    wave[1] = jnp.concatenate(imags, axis=0)

    swap.wait_send()
    other.wait_send()
    for copy in first + second + third + fourth:
        copy.wait_send()
    for i in range(8):
        chip = (2 * c + i // 4) * 32 + z * 4 + i % 4
        for core in range(2):

            @pl.when(jnp.logical_or(chip != s, c != core))
            def _():
                out_copy(i, core, chip).wait_send()


def per_device(frames, aperture, upper_pixels, lower_pixels):
    tiled = frames.reshape(128, 4, 4, 128).transpose(0, 2, 1, 3).reshape(128, 2, 8, 128)
    anywhere = pl.BlockSpec(memory_space=pl.ANY)
    vmem = pl.BlockSpec(memory_space=pltpu.VMEM)
    dma = pltpu.SemaphoreType.DMA
    spectrum, wave = pl.pallas_call(
        kernel,
        out_shape=(jax.ShapeDtypeStruct((2, 4, 256), F32), jax.ShapeDtypeStruct((2, 4, 256), F32)),
        in_specs=[anywhere] * 4,
        out_specs=(vmem, vmem),
        scratch_shapes=[
            pltpu.VMEM((256, 8, 128), F32),
            pltpu.VMEM((1, 256), jnp.int32),
            pltpu.VMEM((64, 128), jnp.int32),
            pltpu.VMEM((64, 128), jnp.int32),
            pltpu.VMEM((128, 128), F32),
            pltpu.VMEM((128, 128), F32),
            pltpu.VMEM((4, 4, 4, 8, 256), F32),
            pltpu.VMEM((3, 4, 4, 8, 256), F32),
            pltpu.VMEM((4, 64, 256), F32),
            pltpu.VMEM((3, 64, 256), F32),
            pltpu.VMEM((8, 8, 256), F32),
            pltpu.VMEM((7, 8, 256), F32),
            pltpu.VMEM((8, 256), F32),
            pltpu.VMEM((8, 256), F32),
            pltpu.VMEM((128, 128), F32),
            pltpu.VMEM((8, 8, 128), F32),
            pltpu.VMEM((8, 8, 128), F32),
            pltpu.VMEM((8, 8, 128), F32),
            pltpu.VMEM((16, 8, 128), F32),
            pltpu.VMEM((256, 512), BF16),
            pltpu.VMEM((256, 512), BF16),
            dma((4,)), dma((4,)), dma((2, 3)), dma((2, 3)), dma((2, 7)), dma((2, 7)), dma((16,)), dma((16,)),
        ],
        compiler_params=pltpu.CompilerParams(
            collective_id=0, has_side_effects=True, vmem_limit_bytes=32 * 1024 * 1024
        ),
    )(tiled, aperture.reshape(1, 256), upper_pixels.T, lower_pixels.T)
    return spectrum, wave.transpose(0, 2, 1)


def solution(mesh):
    placed = (P("det", "scan", None), P(), P(), P())
    return jax.shard_map(
        per_device,
        mesh=mesh,
        in_specs=placed,
        out_specs=(P(None, "scan", "det"), P(None, "det", "scan")),
        check_vma=False,
    )
```

profile of v0, /device:TPU:1, one launch (start us, length us, event | category | flops | bytes accessed | tf_op | source)
XLA Modules:
  0.0 46.2 jit_solution(7846456827785725080)
XLA Ops:
  0.6 0.0 copy-start.3
  0.6 0.7 %copy-done.3 = s32[256]{0:T(256)S(1)} copy-done((s32[256]{0:T(256)S(1)}, s32[256]{0:T(256)}, u32[]{:S(2)}) %copy-start.3) | copy-done | bytes 1048
  1.3 0.0 copy-start
  1.3 1.2 %copy-done = f32[128,4,512]{2,1,0:T(4,128)S(1)} copy-done((f32[128,4,512]{2,1,0:T(4,128)S(1)}, f32[128,4,512]{2,1,0:T(4,128)}, u32[]{:S(2)}) %copy-start) | copy-done | bytes 1048600
  2.5 0.0 copy-start.1
  2.5 0.8 %copy-done.1 = s32[128,64]{0,1:T(8,128)S(1)} copy-done((s32[128,64]{0,1:T(8,128)S(1)}, s32[128,64]{0,1:T(8,128)}, u32[]{:S(2)}) %copy-start.1) | copy-done | bytes 32792
  3.3 0.0 copy-start.2
  3.3 0.8 %copy-done.2 = s32[128,64]{0,1:T(8,128)S(1)} copy-done((s32[128,64]{0,1:T(8,128)S(1)}, s32[128,64]{0,1:T(8,128)}, u32[]{:S(2)}) %copy-start.2) | copy-done | bytes 32792
  4.1 40.9 %shard_map.59 = (f32[2,4,256]{2,1,0:T(4,128)S(1)}, f32[2,4,256]{2,1,0:T(4,128)S(1)}) custom-call(f32[128,2,8,128]{3,2,1,0:T(8,128)S(1)} %bitcast.9, s32[1,256]{1,0:T(1,128)S(1)} %bitcast.13, s32[64,128]{1,0:T(8,128)S(1)} %bitcast.10, s32[64,128]{1,0:T(8,128)S(1)} %bitcast.11), custom_call_target="tpu_custom_call" | custom-call | tf_op jit(solution)/shard_map/pallas_call | solution.py:302
  45.0 0.6 %copy.9 = f32[2,4,256]{2,1,0:T(4,128)} copy(f32[2,4,256]{2,1,0:T(4,128)S(1)} %get-tuple-element.8) | data formatting | bytes 16384
  45.6 0.6 %copy.10 = f32[2,256,4]{1,2,0:T(4,128)} copy(f32[2,256,4]{1,2,0:T(4,128)S(1)} %bitcast.12) | data formatting | bytes 16384
Async XLA Ops:
  0.6 0.7 %copy-start.3 = (s32[256]{0:T(256)S(1)}, s32[256]{0:T(256)}, u32[]{:S(2)}) copy-start(s32[256]{0:T(256)} %param.5) | copy-start | bytes 3076
  1.3 1.2 %copy-start = (f32[128,4,512]{2,1,0:T(4,128)S(1)}, f32[128,4,512]{2,1,0:T(4,128)}, u32[]{:S(2)}) copy-start(f32[128,4,512]{2,1,0:T(4,128)} %param.4) | copy-start | bytes 3145732
  2.5 0.8 %copy-start.1 = (s32[128,64]{0,1:T(8,128)S(1)}, s32[128,64]{0,1:T(8,128)}, u32[]{:S(2)}) copy-start(s32[128,64]{0,1:T(8,128)} %param.6) | copy-start | bytes 98308
  3.3 0.8 %copy-start.2 = (s32[128,64]{0,1:T(8,128)S(1)}, s32[128,64]{0,1:T(8,128)}, u32[]{:S(2)}) copy-start(s32[128,64]{0,1:T(8,128)} %param.7) | copy-start | bytes 98308
where the time goes:
time: 46.4 us; the launch traced here: 46.2 us
  Pallas kernels  40.9 us (88%)
  local copies, waits for them, and re-layouts  4.61 us (10%)
  between operations  0.65 us (1%)
    pallas_call x1, Pallas kernels, per_device(): pl.pallas_call(kernel, out_shape=(jax.ShapeDtypeStruct((2, 4, 256), F32),...  40.9 us
    unnamed x10, local copies, waits for them, and re-layouts  4.61 us

commit v1 on v0

v1 whole, which is shorter than its diff:
```python
import math

import jax
import jax.numpy as jnp
from jax import lax
from jax.experimental import pallas as pl
from jax.experimental.pallas import tpu as pltpu
from jax.sharding import PartitionSpec as P

MESH = pl.DeviceIdType.MESH
F32 = jnp.float32
BF16 = jnp.bfloat16
UNIT = 2.0 * math.pi / 512
SIN = (-1.0 / 6, 1.0 / 120, -1.0 / 5040, 1.0 / 362880, -1.0 / 39916800)


def cos512(m):
    m = m & 511
    t = (128 - jnp.minimum(m, 512 - m)).astype(F32) * UNIT
    t2 = t * t
    poly = jnp.full_like(t, SIN[-1])
    for coefficient in SIN[-2::-1]:
        poly = poly * t2 + coefficient
    return t + t * (t2 * poly)


def split(a):
    high = a.astype(BF16)
    return high, (a - high.astype(F32)).astype(BF16)


def dot(a, b):
    return jnp.dot(a, b, preferred_element_type=F32)


def dot3(a, b_high, b_low):
    rows = a.shape[0]
    a_high, a_low = split(a)
    both = dot(jnp.concatenate((a_high, a_low), axis=0), b_high)
    return both[:rows] + both[rows:] + dot(a_high, b_low)


def iota(shape, dimension):
    return lax.broadcasted_iota(jnp.int32, shape, dimension)


HOPS = (0, 1, 2, 1)
FAR_FIRST = sorted(range(1, 16), key=lambda d: -(HOPS[d % 4] + HOPS[d // 4]))


def kernel(
    frames, aperture, upper, lower,
    spectrum, wave,
    f, ap, up, lo, w, a, r1, zs, r3, t3, r_pair, q, r5, e_high, e_low, back_high, back_low,
    load_sem, pair_sem, sem1, sem3, send5, recv5,
):
    s = lax.axis_index("scan")
    c = lax.axis_index("det")
    y, z, x = s // 32, (s // 4) % 8, s % 4
    me = y * 4 + x

    def plane_peer(d):
        return ((y + d // 4) % 4) * 32 + z * 4 + (x + d % 4) % 4

    def z_peer(d):
        return s + ((z + d) % 8 - z) * 4

    loads = [
        pltpu.make_async_copy(upper, up, load_sem.at[0]),
        pltpu.make_async_copy(lower, lo, load_sem.at[1]),
        pltpu.make_async_copy(aperture, ap, load_sem.at[2]),
        pltpu.make_async_copy(frames.at[:, c], f.at[pl.ds(c * 128, 128)], load_sem.at[3]),
    ]
    for load in loads:
        load.start()

    barrier = pltpu.get_barrier_semaphore()

    def greet(scan, det):
        pl.semaphore_signal(barrier, inc=1, device_id=(scan, det), device_id_type=MESH)

    for d in (4, 3, 5, 2, 6, 1, 7):
        greet(z_peer(d), c)
    for d in FAR_FIRST:
        greet(plane_peer(d), c)
    greet(s, 1 - c)
    home = y // 2 == c

    @pl.when(jnp.logical_not(home))
    def _():
        for d in FAR_FIRST:
            greet(plane_peer(d), 1 - c)

    pl.semaphore_wait(barrier, 31 - jnp.where(home, 1, 0))

    swap = pltpu.make_async_remote_copy(
        src_ref=frames.at[:, 1 - c], dst_ref=f.at[pl.ds(c * 128, 128)],
        send_sem=pair_sem.at[0], recv_sem=pair_sem.at[1], device_id=(s, 1 - c), device_id_type=MESH,
    )
    swap.start()

    for load in loads[:3]:
        load.wait()
    pixel = iota((256, 128), 0)

    def count(j, total):
        plus = jnp.where(up[pl.ds(j, 1), :] == pixel, 1, 0)
        return total + plus - jnp.where(lo[pl.ds(j, 1), :] == pixel, 1, 0)

    counts = lax.fori_loop(0, 64, count, jnp.zeros((256, 128), jnp.int32))
    scaled = counts.astype(F32) * (64**-0.5 / 512)
    w[:128] = scaled[:128].T
    w[128:] = scaled[128:].T

    def weights(core):
        tiles = [w[pl.ds(core * 128 + 32 * (i // 4) + i % 4, 8, stride=4), :] for i in range(16)]
        inside = jnp.where(core == 0, ap[:, :128], ap[:, 128:]).astype(F32)
        weight = (jnp.concatenate(tiles, axis=0) * inside).astype(BF16)
        return jnp.concatenate((weight, weight), axis=1)

    flat = f.reshape(2048, 128)

    def weighted(weight, core, i):
        rows = [flat[pl.ds(core * 1024 + 4 * j + i, 128, stride=8), :] for j in range(2)]
        high, low = split(jnp.concatenate(rows, axis=1))
        return dot(weight, jnp.concatenate((high, low), axis=0)).reshape(16, 8, 256)

    near, far = weights(c), weights(1 - c)
    loads[3].wait()
    for i in range(4):
        a[:, i] = weighted(near, c, i)
    swap.wait_recv()

    def first_copy(d, h):
        target = ((y + d // 4) % 4) * 4 + (x + d % 4) % 4
        return pltpu.make_async_remote_copy(
            src_ref=a.at[target, pl.ds(2 * h, 2)], dst_ref=r1.at[d, pl.ds(2 * h, 2)],
            send_sem=sem1.at[0, h, d], recv_sem=sem1.at[1, h, d],
            device_id=(plane_peer(d), c), device_id_type=MESH,
        )

    for h in range(2):
        for i in range(2 * h, 2 * h + 2):
            a[:, i] = a[:, i] + weighted(far, 1 - c, i)
        for d in FAR_FIRST:
            first_copy(d, h).start()

    row, column = iota((64, 512), 0), iota((64, 512), 1)
    slot = column // 32
    chip = ((y - slot // 4) & 3) * 32 + 4 * z + ((x - slot % 4) & 3)
    place = 4 * chip + (column // 8) % 4
    block = y * 32 + x + 4 * (row // 8)
    left = cos512((4 * block + row % 4) * place + 32 * (row % 8 - row % 4))
    left_high, left_low = split(jnp.where(row // 8 == column % 8, left, 0.0))

    frequency = iota((256, 512), 1)
    wide = frequency % 256 + 256 * c
    table_high, table_low = split(cos512(wide * iota((256, 512), 0) - 128 * (frequency // 256)))
    e_high[...] = table_high
    e_low[...] = table_low

    n, source = iota((1024, 256), 1), iota((1024, 256), 0)
    source_block = (source // 256) * 32 + (source // 64) % 4 + 4 * ((source // 8) % 8)
    table_high, table_low = split(cos512(4 * source_block * (n % 128) - 128 * (n // 128)))
    back_high[...] = table_high
    back_low[...] = table_low

    part = jnp.zeros((64, 256), F32)
    for g in range(2):
        rows = []
        for d in range(8 * g, 8 * g + 8):
            if d:
                for h in range(2):
                    first_copy(d, h).wait_recv()
                rows.append(r1[d].reshape(32, 256))
            else:
                rows.append(a[me].reshape(32, 256))
        right_high, right_low = split(jnp.concatenate(rows, axis=0))
        columns = slice(256 * g, 256 * g + 256)
        both = dot(jnp.concatenate((left_high[:, columns], left_low[:, columns]), axis=0), right_high)
        part = part + (both[:64] + both[64:]) + dot(left_high[:, columns], right_low)

    turned = jnp.concatenate((part[:, :128], part[:, 128:]), axis=0).T
    for i in range(8):
        zs[i, :8] = part[8 * i : 8 * i + 8, :128]
        zs[i, 8:16] = part[8 * i : 8 * i + 8, 128:]
        zs[i, 16:] = turned[16 * i : 16 * i + 16]

    def third_copy(d):
        return pltpu.make_async_remote_copy(
            src_ref=zs.at[(z + d) % 8], dst_ref=r3.at[d], send_sem=sem3.at[0, d], recv_sem=sem3.at[1, d],
            device_id=(z_peer(d), c), device_id_type=MESH,
        )

    for d in (4, 3, 5, 2, 6, 1, 7):
        third_copy(d).start()
    total = zs[z]
    for d in (1, 7, 2, 6, 3, 5, 4):
        third_copy(d).wait_recv()
        total = total + r3[d]

    for i in range(4):
        q[i] = total[16 + 4 * i : 20 + 4 * i]

    def out_copy(i, core):
        chip = (2 * c + i // 4) * 32 + z * 4 + i % 4
        copy = pltpu.make_async_remote_copy(
            src_ref=q.at[i % 4], dst_ref=r5.at[me], send_sem=send5.at[2 * i + core], recv_sem=recv5.at[me],
            device_id=(chip, core), device_id_type=MESH,
        )
        return copy, jnp.logical_and(chip == s, c == core)

    for i in range(8):
        for core in range(2):
            copy, mine = out_copy(i, core)

            @pl.when(jnp.logical_not(mine))
            def _():
                copy.start()

            @pl.when(mine)
            def _():
                pltpu.make_async_copy(q.at[i % 4], r5.at[me], recv5.at[me]).start()

    band = jnp.concatenate((total[:8], total[8:16]), axis=1)
    t3[...] = band
    other = pltpu.make_async_remote_copy(
        src_ref=t3, dst_ref=r_pair, send_sem=pair_sem.at[2], recv_sem=pair_sem.at[3],
        device_id=(s, 1 - c), device_id_type=MESH,
    )
    other.start()
    lane, rho = iota((8, 256), 1), iota((8, 256), 0)
    angle = (rho % 4) * (lane + 256 * c) + 128 * (rho // 4)
    turn_real, turn_imag = cos512(angle), cos512(angle - 128)
    other.wait_recv()
    sums = dot3(jnp.concatenate((band, r_pair[...]), axis=0), e_high[...], e_low[...])
    sign = (1 - 2 * (lane % 2)).astype(F32)
    near, far = jnp.where(c == 0, 1.0, sign), jnp.where(c == 0, sign, 1.0)
    cosine = near * sums[:8, :256] + far * sums[8:, :256]
    sine = near * sums[:8, 256:] + far * sums[8:, 256:]
    side = jnp.where(rho < 4, -1.0, 1.0)
    result = cosine - side * jnp.concatenate((sine[4:], sine[:4]), axis=0)
    spectrum[0] = result[:4]
    spectrum[1] = result[4:]

    for i in range(16):
        pltpu.make_async_copy(q.at[0], r5.at[i], recv5.at[i]).wait()
    low_half = iota((4, 128), 1) < 64
    upper_y = y % 2 == 1
    mask = iota((8, 128), 0) == iota((8, 128), 1) % 8
    columns = []
    for j in range(8):
        even, odd = r5[2 * j], r5[2 * j + 1]
        even = jnp.where(upper_y, pltpu.roll(even, 64, 1), even)
        odd = jnp.where(upper_y, odd, pltpu.roll(odd, 64, 1))
        pair = jnp.where(low_half, even, odd)
        columns.append(jnp.concatenate([jnp.where(mask, pair[i : i + 1], 0.0) for i in range(4)], axis=0))
    moved = dot3(jnp.concatenate(columns, axis=1), back_high[...], back_low[...])
    reals, imags = [], []
    for i in range(4):
        tile = moved[8 * i : 8 * i + 8]
        sine = tile[:, 128:]
        pair = tile[:, :128] + side[:, :128] * jnp.concatenate((sine[4:], sine[:4]), axis=0)
        twice = jnp.concatenate((pair, pair), axis=1)
        reals.append(jnp.sum(twice * turn_real, axis=0, keepdims=True))
        imags.append(jnp.sum(twice * turn_imag, axis=0, keepdims=True))
    wave[0] = jnp.concatenate(reals, axis=0)
    wave[1] = jnp.concatenate(imags, axis=0)

    swap.wait_send()
    other.wait_send()
    for d in range(1, 16):
        first_copy(d, 0).wait_send()
        first_copy(d, 1).wait_send()
    for d in range(1, 8):
        third_copy(d).wait_send()
    for i in range(8):
        for core in range(2):
            copy, mine = out_copy(i, core)

            @pl.when(jnp.logical_not(mine))
            def _():
                copy.wait_send()


def per_device(frames, aperture, upper_pixels, lower_pixels):
    tiled = frames.reshape(128, 4, 4, 128).transpose(0, 2, 1, 3).reshape(128, 2, 8, 128)
    hbm = pl.BlockSpec(memory_space=pltpu.HBM)
    vmem = pl.BlockSpec(memory_space=pltpu.VMEM)
    dma = pltpu.SemaphoreType.DMA
    spectrum, wave = pl.pallas_call(
        kernel,
        out_shape=(jax.ShapeDtypeStruct((2, 4, 256), F32), jax.ShapeDtypeStruct((2, 4, 256), F32)),
        in_specs=[hbm] * 4,
        out_specs=(vmem, vmem),
        scratch_shapes=[
            pltpu.VMEM((256, 8, 128), F32),
            pltpu.VMEM((1, 256), jnp.int32),
            pltpu.VMEM((64, 128), jnp.int32),
            pltpu.VMEM((64, 128), jnp.int32),
            pltpu.VMEM((256, 128), F32),
            pltpu.VMEM((16, 4, 8, 256), F32),
            pltpu.VMEM((16, 4, 8, 256), F32),
            pltpu.VMEM((8, 32, 128), F32),
            pltpu.VMEM((8, 32, 128), F32),
            pltpu.VMEM((8, 256), F32),
            pltpu.VMEM((8, 256), F32),
            pltpu.VMEM((4, 4, 128), F32),
            pltpu.VMEM((16, 4, 128), F32),
            pltpu.VMEM((256, 512), BF16),
            pltpu.VMEM((256, 512), BF16),
            pltpu.VMEM((1024, 256), BF16),
            pltpu.VMEM((1024, 256), BF16),
            dma((4,)), dma((4,)), dma((2, 2, 16)), dma((2, 8)), dma((16,)), dma((16,)),
        ],
        compiler_params=pltpu.CompilerParams(
            collective_id=0, has_side_effects=True, vmem_limit_bytes=56 * 1024 * 1024
        ),
    )(tiled, aperture.reshape(1, 256), upper_pixels.T, lower_pixels.T)
    return spectrum, wave.transpose(0, 2, 1)


def solution(mesh):
    placed = (P("det", "scan", None), P(), P(), P())
    return jax.shard_map(
        per_device,
        mesh=mesh,
        in_specs=placed,
        out_specs=(P(None, "scan", "det"), P(None, "det", "scan")),
        check_vma=False,
    )
```

time: 46.4 us -> 39.4 us (0.85)
  Pallas kernels: 40.9 us -> 36.7 us
  local copies, waits for them, and re-layouts: 4.61 us -> 1.9 us
    pallas_call x1, Pallas kernels: 40.9 us -> 36.7 us  [per_device(): pl.pallas_call(kernel, out_shape=(jax.ShapeDtypeStruct((2, 4, 256), F32),...]
    unnamed x10 -> x4, local copies, waits for them, and re-layouts: 4.61 us -> 1.9 us
where the time goes in v1:
time: 39.4 us; the launch traced here: 39.2 us
  Pallas kernels  36.7 us (93%)
  local copies, waits for them, and re-layouts  1.9 us (5%)
  between operations  0.65 us (2%)
    pallas_call x1, Pallas kernels, per_device(): pl.pallas_call(kernel, out_shape=(jax.ShapeDtypeStruct((2, 4, 256), F32),...  36.7 us
    unnamed x4, local copies, waits for them, and re-layouts  1.9 us

profile of v1, /device:TPU:1, one launch (start us, length us, event | category | flops | bytes accessed | tf_op | source)
XLA Modules:
  0.0 39.2 jit_solution(10054948507910099228)
XLA Ops:
  0.6 36.7 %shard_map.59 = (f32[2,4,256]{2,1,0:T(4,128)}, f32[2,4,256]{2,1,0:T(4,128)}) custom-call(f32[128,2,8,128]{3,2,1,0:T(8,128)} %bitcast.9, s32[1,256]{1,0:T(1,128)} %bitcast.13, s32[64,128]{1,0:T(8,128)} %bitcast.10, s32[64,128]{1,0:T(8,128)} %bitcast.11), custom_call_target="tpu_custom_call" | custom-call | tf_op jit(solution)/shard_map/pallas_call | solution.py:291
  37.3 0.0 copy-start
  37.3 1.3 %copy.9 = f32[2,4,256]{2,1,0:T(4,128)} copy(f32[2,4,256]{2,1,0:T(4,128)} %get-tuple-element.8) | data formatting | bytes 16384
  38.6 0.0 copy-done
  38.6 0.6 %copy.10 = f32[2,256,4]{1,2,0:T(4,128)} copy(f32[2,256,4]{1,2,0:T(4,128)S(1)} %bitcast.12) | data formatting | bytes 16384
Async XLA Ops:
  37.3 1.3 %copy-start = (f32[2,4,256]{2,1,0:T(4,128)S(1)}, f32[2,4,256]{2,1,0:T(4,128)}, u32[]{:S(2)}) copy-start(f32[2,4,256]{2,1,0:T(4,128)} %get-tuple-element.5) | copy-start | bytes 24580

commit v2 on v1

--- a/solution.py
+++ b/solution.py
@@ -50,9 +50,9 @@
 
 def kernel(
     frames, aperture, upper, lower,
-    spectrum, wave,
-    f, ap, up, lo, w, a, r1, zs, r3, t3, r_pair, q, r5, e_high, e_low, back_high, back_low,
-    load_sem, pair_sem, sem1, sem3, send5, recv5,
+    out,
+    f, ap, up, lo, w, a, b, r1, zs, r3, t3, r_pair, q, r5, e_high, e_low, back_high, back_low,
+    load_sem, swap_sem, pair_sem, sem1, sem3, send5, recv5,
 ):
     s = lax.axis_index("scan")
     c = lax.axis_index("det")
@@ -69,7 +69,7 @@
         pltpu.make_async_copy(upper, up, load_sem.at[0]),
         pltpu.make_async_copy(lower, lo, load_sem.at[1]),
         pltpu.make_async_copy(aperture, ap, load_sem.at[2]),
-        pltpu.make_async_copy(frames.at[:, c], f.at[pl.ds(c * 128, 128)], load_sem.at[3]),
+        pltpu.make_async_copy(frames, f, load_sem.at[3]),
     ]
     for load in loads:
         load.start()
@@ -79,71 +79,79 @@
     def greet(scan, det):
         pl.semaphore_signal(barrier, inc=1, device_id=(scan, det), device_id_type=MESH)
 
-    for d in (4, 3, 5, 2, 6, 1, 7):
-        greet(z_peer(d), c)
-    for d in FAR_FIRST:
-        greet(plane_peer(d), c)
+    home = y // 2 == c
+    for hops in range(4, 0, -1):
+        for d in range(1, 8):
+            if min(d, 8 - d) == hops:
+                greet(z_peer(d), c)
+        peers = [d for d in FAR_FIRST if HOPS[d % 4] + HOPS[d // 4] == hops]
+        for d in peers:
+            greet(plane_peer(d), c)
+
+        @pl.when(jnp.logical_not(home))
+        def _():
+            for d in peers:
+                greet(plane_peer(d), 1 - c)
+
     greet(s, 1 - c)
-    home = y // 2 == c
-
-    @pl.when(jnp.logical_not(home))
-    def _():
-        for d in FAR_FIRST:
-            greet(plane_peer(d), 1 - c)
-
-    pl.semaphore_wait(barrier, 31 - jnp.where(home, 1, 0))
-
-    swap = pltpu.make_async_remote_copy(
-        src_ref=frames.at[:, 1 - c], dst_ref=f.at[pl.ds(c * 128, 128)],
-        send_sem=pair_sem.at[0], recv_sem=pair_sem.at[1], device_id=(s, 1 - c), device_id_type=MESH,
-    )
-    swap.start()
 
     for load in loads[:3]:
         load.wait()
-    pixel = iota((256, 128), 0)
+    pixel = (iota((128, 128), 0) + 128 * c).astype(F32).astype(BF16)
+    one, none = jnp.ones((128, 128), BF16), jnp.zeros((128, 128), BF16)
+
+    def row_of(ref, j):
+        return jnp.broadcast_to(ref[pl.ds(j, 1), :], (128, 128)).astype(F32).astype(BF16)
 
     def count(j, total):
-        plus = jnp.where(up[pl.ds(j, 1), :] == pixel, 1, 0)
-        return total + plus - jnp.where(lo[pl.ds(j, 1), :] == pixel, 1, 0)
-
-    counts = lax.fori_loop(0, 64, count, jnp.zeros((256, 128), jnp.int32))
-    scaled = counts.astype(F32) * (64**-0.5 / 512)
-    w[:128] = scaled[:128].T
-    w[128:] = scaled[128:].T
-
-    def weights(core):
-        tiles = [w[pl.ds(core * 128 + 32 * (i // 4) + i % 4, 8, stride=4), :] for i in range(16)]
-        inside = jnp.where(core == 0, ap[:, :128], ap[:, 128:]).astype(F32)
-        weight = (jnp.concatenate(tiles, axis=0) * inside).astype(BF16)
-        return jnp.concatenate((weight, weight), axis=1)
+        total = total + jnp.where(row_of(up, j) == pixel, one, none)
+        return total - jnp.where(row_of(lo, j) == pixel, one, none)
+
+    counts = lax.fori_loop(0, 64, count, none, unroll=4)
+    w[...] = (counts.astype(F32) * (64**-0.5 / 512)).T
+    tiles = [w[pl.ds(32 * (i // 4) + i % 4, 8, stride=4), :] for i in range(16)]
+    inside = jnp.where(c == 0, ap[:, :128], ap[:, 128:]).astype(F32)
+    weight = (jnp.concatenate(tiles, axis=0) * inside).astype(BF16)
+    weight = jnp.concatenate((weight, weight), axis=1)
 
     flat = f.reshape(2048, 128)
 
-    def weighted(weight, core, i):
-        rows = [flat[pl.ds(core * 1024 + 4 * j + i, 128, stride=8), :] for j in range(2)]
-        high, low = split(jnp.concatenate(rows, axis=1))
-        return dot(weight, jnp.concatenate((high, low), axis=0)).reshape(16, 8, 256)
-
-    near, far = weights(c), weights(1 - c)
+    def weighted(half):
+        for i in range(4):
+            rows = [flat[pl.ds(8 * half + 4 * j + i, 128, stride=16), :] for j in range(2)]
+            high, low = split(jnp.concatenate(rows, axis=1))
+            sums = dot(weight, jnp.concatenate((high, low), axis=0))
+            a[half, :, i] = sums.reshape(16, 8, 256)
+
     loads[3].wait()
-    for i in range(4):
-        a[:, i] = weighted(near, c, i)
-    swap.wait_recv()
-
-    def first_copy(d, h):
-        target = ((y + d // 4) % 4) * 4 + (x + d % 4) % 4
+    weighted(1 - c)
+
+    pl.semaphore_wait(barrier, 31 - jnp.where(home, 1, 0))
+
+    def plane_index(d):
+        return ((y + d // 4) % 4) * 4 + (x + d % 4) % 4
+
+    def swap_copy(d):
         return pltpu.make_async_remote_copy(
-            src_ref=a.at[target, pl.ds(2 * h, 2)], dst_ref=r1.at[d, pl.ds(2 * h, 2)],
-            send_sem=sem1.at[0, h, d], recv_sem=sem1.at[1, h, d],
+            src_ref=a.at[1 - c, plane_index(d)], dst_ref=b.at[d], send_sem=swap_sem.at[0, d], recv_sem=swap_sem.at[1, d],
+            device_id=(s, 1 - c), device_id_type=MESH,
+        )
+
+    for d in FAR_FIRST + [0]:
+        swap_copy(d).start()
+    weighted(c)
+
+    def first_copy(d):
+        return pltpu.make_async_remote_copy(
+            src_ref=b.at[d], dst_ref=r1.at[d], send_sem=sem1.at[0, d], recv_sem=sem1.at[1, d],
             device_id=(plane_peer(d), c), device_id_type=MESH,
         )
 
-    for h in range(2):
-        for i in range(2 * h, 2 * h + 2):
-            a[:, i] = a[:, i] + weighted(far, 1 - c, i)
-        for d in FAR_FIRST:
-            first_copy(d, h).start()
+    for d in FAR_FIRST + [0]:
+        swap_copy(d).wait_recv()
+        b[d] = b[d] + a[c, plane_index(d)]
+        if d:
+            first_copy(d).start()
 
     row, column = iota((64, 512), 0), iota((64, 512), 1)
     slot = column // 32
@@ -170,11 +178,10 @@
         rows = []
         for d in range(8 * g, 8 * g + 8):
             if d:
-                for h in range(2):
-                    first_copy(d, h).wait_recv()
+                first_copy(d).wait_recv()
                 rows.append(r1[d].reshape(32, 256))
             else:
-                rows.append(a[me].reshape(32, 256))
+                rows.append(b[0].reshape(32, 256))
         right_high, right_low = split(jnp.concatenate(rows, axis=0))
         columns = slice(256 * g, 256 * g + 256)
         both = dot(jnp.concatenate((left_high[:, columns], left_low[:, columns]), axis=0), right_high)
@@ -186,21 +193,29 @@
         zs[i, 8:16] = part[8 * i : 8 * i + 8, 128:]
         zs[i, 16:] = turned[16 * i : 16 * i + 16]
 
-    def third_copy(d):
+    def third_copy(d, h):
+        rows = pl.ds(16 * h, 16)
         return pltpu.make_async_remote_copy(
-            src_ref=zs.at[(z + d) % 8], dst_ref=r3.at[d], send_sem=sem3.at[0, d], recv_sem=sem3.at[1, d],
+            src_ref=zs.at[(z + d) % 8, rows], dst_ref=r3.at[d, rows],
+            send_sem=sem3.at[0, h, d], recv_sem=sem3.at[1, h, d],
             device_id=(z_peer(d), c), device_id_type=MESH,
         )
 
-    for d in (4, 3, 5, 2, 6, 1, 7):
-        third_copy(d).start()
-    total = zs[z]
-    for d in (1, 7, 2, 6, 3, 5, 4):
-        third_copy(d).wait_recv()
-        total = total + r3[d]
-
+    def z_sum(h):
+        rows = pl.ds(16 * h, 16)
+        total = zs[z, rows]
+        for d in (1, 7, 2, 6, 3, 5, 4):
+            third_copy(d, h).wait_recv()
+            total = total + r3[d, rows]
+        return total
+
+    for h in (1, 0):
+        for d in (4, 3, 5, 2, 6, 1, 7):
+            third_copy(d, h).start()
+
+    total = z_sum(1)
     for i in range(4):
-        q[i] = total[16 + 4 * i : 20 + 4 * i]
+        q[i] = total[4 * i : 4 * i + 4]
 
     def out_copy(i, core):
         chip = (2 * c + i // 4) * 32 + z * 4 + i % 4
@@ -222,10 +237,11 @@
             def _():
                 pltpu.make_async_copy(q.at[i % 4], r5.at[me], recv5.at[me]).start()
 
-    band = jnp.concatenate((total[:8], total[8:16]), axis=1)
+    total = z_sum(0)
+    band = jnp.concatenate((total[:8], total[8:]), axis=1)
     t3[...] = band
     other = pltpu.make_async_remote_copy(
-        src_ref=t3, dst_ref=r_pair, send_sem=pair_sem.at[2], recv_sem=pair_sem.at[3],
+        src_ref=t3, dst_ref=r_pair, send_sem=pair_sem.at[0], recv_sem=pair_sem.at[1],
         device_id=(s, 1 - c), device_id_type=MESH,
     )
     other.start()
@@ -240,8 +256,8 @@
     sine = near * sums[:8, 256:] + far * sums[8:, 256:]
     side = jnp.where(rho < 4, -1.0, 1.0)
     result = cosine - side * jnp.concatenate((sine[4:], sine[:4]), axis=0)
-    spectrum[0] = result[:4]
-    spectrum[1] = result[4:]
+    out[0] = result[:4]
+    out[1] = result[4:]
 
     for i in range(16):
         pltpu.make_async_copy(q.at[0], r5.at[i], recv5.at[i]).wait()
@@ -264,16 +280,17 @@
         twice = jnp.concatenate((pair, pair), axis=1)
         reals.append(jnp.sum(twice * turn_real, axis=0, keepdims=True))
         imags.append(jnp.sum(twice * turn_imag, axis=0, keepdims=True))
-    wave[0] = jnp.concatenate(reals, axis=0)
-    wave[1] = jnp.concatenate(imags, axis=0)
-
-    swap.wait_send()
+    out[2] = jnp.concatenate(reals, axis=0)
+    out[3] = jnp.concatenate(imags, axis=0)
+
+    for d in range(16):
+        swap_copy(d).wait_send()
     other.wait_send()
     for d in range(1, 16):
-        first_copy(d, 0).wait_send()
-        first_copy(d, 1).wait_send()
+        first_copy(d).wait_send()
     for d in range(1, 8):
-        third_copy(d).wait_send()
+        third_copy(d, 0).wait_send()
+        third_copy(d, 1).wait_send()
     for i in range(8):
         for core in range(2):
             copy, mine = out_copy(i, core)
@@ -285,20 +302,21 @@
 
 def per_device(frames, aperture, upper_pixels, lower_pixels):
     tiled = frames.reshape(128, 4, 4, 128).transpose(0, 2, 1, 3).reshape(128, 2, 8, 128)
+    operands = (tiled, aperture.reshape(1, 256), upper_pixels.T, lower_pixels.T)
     hbm = pl.BlockSpec(memory_space=pltpu.HBM)
-    vmem = pl.BlockSpec(memory_space=pltpu.VMEM)
     dma = pltpu.SemaphoreType.DMA
-    spectrum, wave = pl.pallas_call(
+    both = pl.pallas_call(
         kernel,
-        out_shape=(jax.ShapeDtypeStruct((2, 4, 256), F32), jax.ShapeDtypeStruct((2, 4, 256), F32)),
+        out_shape=pltpu.VMEM((4, 4, 256), F32),
         in_specs=[hbm] * 4,
-        out_specs=(vmem, vmem),
+        out_specs=pl.BlockSpec(memory_space=pltpu.VMEM),
         scratch_shapes=[
-            pltpu.VMEM((256, 8, 128), F32),
+            pltpu.VMEM((128, 2, 8, 128), F32),
             pltpu.VMEM((1, 256), jnp.int32),
             pltpu.VMEM((64, 128), jnp.int32),
             pltpu.VMEM((64, 128), jnp.int32),
-            pltpu.VMEM((256, 128), F32),
+            pltpu.VMEM((128, 128), F32),
+            pltpu.VMEM((2, 16, 4, 8, 256), F32),
             pltpu.VMEM((16, 4, 8, 256), F32),
             pltpu.VMEM((16, 4, 8, 256), F32),
             pltpu.VMEM((8, 32, 128), F32),
@@ -311,13 +329,13 @@
             pltpu.VMEM((256, 512), BF16),
             pltpu.VMEM((1024, 256), BF16),
             pltpu.VMEM((1024, 256), BF16),
-            dma((4,)), dma((4,)), dma((2, 2, 16)), dma((2, 8)), dma((16,)), dma((16,)),
+            dma((4,)), dma((2, 16)), dma((2,)), dma((2, 16)), dma((2, 2, 8)), dma((16,)), dma((16,)),
         ],
         compiler_params=pltpu.CompilerParams(
-            collective_id=0, has_side_effects=True, vmem_limit_bytes=56 * 1024 * 1024
+            collective_id=0, has_side_effects=True, vmem_limit_bytes=32 * 1024 * 1024
         ),
-    )(tiled, aperture.reshape(1, 256), upper_pixels.T, lower_pixels.T)
-    return spectrum, wave.transpose(0, 2, 1)
+    )(*[pltpu.with_memory_space_constraint(operand, pltpu.HBM) for operand in operands])
+    return both[:2], both[2:].transpose(0, 2, 1)
 
 
 def solution(mesh):

time: 39.4 us -> 33.4 us (0.85)
  Pallas kernels: 36.7 us -> 32.1 us
  local copies, waits for them, and re-layouts: 1.9 us -> 0.61 us
    pallas_call x1, Pallas kernels: 36.7 us -> 32.1 us  [per_device(): pl.pallas_call(kernel, out_shape=pltpu.VMEM((4, 4, 256), F32), in_specs=[...]
    unnamed x4 -> x0, local copies, waits for them, and re-layouts: 1.9 us -> none
    transpose x0 -> x1, local copies, waits for them, and re-layouts: none -> 0.61 us  [per_device(): return (both[:2], both[2:].transpose(0, 2, 1))]
where the time goes in v2:
time: 33.4 us; the launch traced here: 33.3 us
  Pallas kernels  32.1 us (96%)
  between operations  0.64 us (2%)
  local copies, waits for them, and re-layouts  0.61 us (2%)
    pallas_call x1, Pallas kernels, per_device(): pl.pallas_call(kernel, out_shape=pltpu.VMEM((4, 4, 256), F32), in_specs=[...  32.1 us

profile of v2, /device:TPU:1, one launch (start us, length us, event | category | flops | bytes accessed | tf_op | source)
XLA Modules:
  0.0 33.3 jit_solution(17252331608181159890)
XLA Ops:
  0.6 32.1 %shard_map.59 = f32[4,4,256]{2,1,0:T(4,128)S(1)} custom-call(f32[128,2,8,128]{3,2,1,0:T(8,128)} %bitcast.10, s32[1,256]{1,0:T(1,128)} %bitcast.13, s32[64,128]{1,0:T(8,128)} %bitcast.11, s32[64,128]{1,0:T(8,128)} %bitcast.12), custom_call_target="tpu_custom_call" | custom-call | tf_op jit(solution)/shard_map/pallas_call | solution.py:308
  32.7 0.6 %slice_bitcast_fusion = (f32[2,256,4]{1,2,0:T(4,128)}, f32[2,4,256]{2,1,0:T(4,128)}) fusion(f32[4,4,256]{2,1,0:T(4,128)S(1)} %shard_map.59), kind=kLoop, calls=%fused_computation | loop fusion | bytes 32768 | tf_op jit(solution)/shard_map/transpose | solution.py:338

commit v3 on v2

v3 whole, which is shorter than its diff:
```python
import math

import jax
import jax.numpy as jnp
from jax import lax
from jax.experimental import pallas as pl
from jax.experimental.pallas import tpu as pltpu
from jax.sharding import PartitionSpec as P

MESH = pl.DeviceIdType.MESH
F32 = jnp.float32
BF16 = jnp.bfloat16
UNIT = 2.0 * math.pi / 512
SIN = (-1.0 / 6, 1.0 / 120, -1.0 / 5040, 1.0 / 362880, -1.0 / 39916800)


def cos512(m):
    m = m & 511
    t = (128 - jnp.minimum(m, 512 - m)).astype(F32) * UNIT
    t2 = t * t
    poly = jnp.full_like(t, SIN[-1])
    for coefficient in SIN[-2::-1]:
        poly = poly * t2 + coefficient
    return t + t * (t2 * poly)


def split(a):
    high = a.astype(BF16)
    return high, (a - high.astype(F32)).astype(BF16)


def dot(a, b):
    return jnp.dot(a, b, preferred_element_type=F32)


def dot3(a, b_high, b_low):
    rows = a.shape[0]
    a_high, a_low = split(a)
    both = dot(jnp.concatenate((a_high, a_low), axis=0), b_high)
    return both[:rows] + both[rows:] + dot(a_high, b_low)


def iota(shape, dimension):
    return lax.broadcasted_iota(jnp.int32, shape, dimension)


LOADS = 4


def kernel(
    frames, aperture, upper, lower,
    out,
    f, ap, up, lo, w, a, b, r1, zs, r3, q, r5, t, r6, e_high, e_low, back_high, back_low,
    load_sem, swap_sem, sem1, sem3, send5, recv5, send6, recv6,
):
    s = lax.axis_index("scan")
    c = lax.axis_index("det")
    y, z, x = s // 32, (s // 4) % 8, s % 4
    me = y * 4 + x
    home = y // 2 == c

    def chip_at(cy, cx):
        return cy * 32 + z * 4 + cx

    first_row = jnp.where(home, 1 - y % 2, y % 2)
    TARGETS = [(dx, j, core) for dx in (2, 1, 3, 0) for j in range(2) for core in range(2)]

    def target(dx, j):
        return (x + dx) % 4, first_row * (1 - j) + (1 - first_row) * j

    def z_peer(d):
        return s + ((z + d) % 8 - z) * 4

    loads = [
        pltpu.make_async_copy(upper, up, load_sem.at[0]),
        pltpu.make_async_copy(lower, lo, load_sem.at[1]),
        pltpu.make_async_copy(aperture, ap, load_sem.at[2]),
    ]
    for i in range(LOADS):
        pixels = pl.ds(i * (128 // LOADS), 128 // LOADS)
        loads.append(pltpu.make_async_copy(frames.at[pixels], f.at[pixels], load_sem.at[3 + i]))
    for load in loads:
        load.start()

    barrier = pltpu.get_barrier_semaphore()

    def greet(scan, det):
        pl.semaphore_signal(barrier, inc=1, device_id=(scan, det), device_id_type=MESH)

    for d in (4, 3, 5, 2, 6, 1, 7):
        greet(z_peer(d), c)
    for dx in (2, 1, 3, 0):
        for dy in (2, 1, 3, 0):

            @pl.when(jnp.logical_or(jnp.logical_not(home), dx + dy > 0))
            def _():
                greet(chip_at((y + dy) % 4, (x + dx) % 4), y // 2)

        @pl.when(jnp.logical_or(home, dx > 0))
        def _():
            greet(chip_at(y, (x + dx) % 4), 1 - y // 2)

    for load in loads[:3]:
        load.wait()
    pixel = (iota((128, 128), 0) + 128 * c).astype(F32).astype(BF16)
    one, none = jnp.ones((128, 128), BF16), jnp.zeros((128, 128), BF16)

    def row_of(ref, j):
        return jnp.broadcast_to(ref[pl.ds(j, 1), :], (128, 128)).astype(F32).astype(BF16)

    def count(j, total):
        total = total + jnp.where(row_of(up, j) == pixel, one, none)
        return total - jnp.where(row_of(lo, j) == pixel, one, none)

    counts = lax.fori_loop(0, 64, count, none, unroll=4)
    w[...] = (counts.astype(F32) * (64**-0.5 / 512)).T
    tiles = [w[pl.ds(32 * (i % 4) + i // 4, 8, stride=4), :] for i in range(16)]
    inside = jnp.where(c == 0, ap[:, :128], ap[:, 128:]).astype(F32)
    weight = (jnp.concatenate(tiles, axis=0) * inside).astype(BF16)
    weight = jnp.concatenate((weight, weight), axis=1)

    flat = f.reshape(2048, 128)

    def weighted(half):
        for i in range(4):
            rows = [flat[pl.ds(8 * half + 4 * j + i, 128, stride=16), :] for j in range(2)]
            high, low = split(jnp.concatenate(rows, axis=1))
            sums = dot(weight, jnp.concatenate((high, low), axis=0))
            for j in range(2):
                a[half, j, :, :, i] = sums[:, 128 * j : 128 * j + 128].reshape(4, 2, 16, 128)

    for load in loads[3:]:
        load.wait()
    weighted(1 - c)

    pl.semaphore_wait(barrier, jnp.where(home, 22, 30))

    def swap_copy(i):
        dx, j, core = TARGETS[i]
        cx, row = target(dx, j)
        far_row = jnp.where(home, y % 2, 1 - y % 2) * (1 - j) + jnp.where(home, 1 - y % 2, y % 2) * j
        return pltpu.make_async_remote_copy(
            src_ref=a.at[1 - c, far_row, cx, core], dst_ref=b.at[i],
            send_sem=swap_sem.at[0, i], recv_sem=swap_sem.at[1, i], device_id=(s, 1 - c), device_id_type=MESH,
        )

    for i in range(16):
        swap_copy(i).start()
    weighted(c)

    def first_copy(i):
        dx, j, core = TARGETS[i]
        cx, row = target(dx, j)
        chip = chip_at(2 * c + row, cx)
        copy = pltpu.make_async_remote_copy(
            src_ref=b.at[i], dst_ref=r1.at[me], send_sem=sem1.at[0, i], recv_sem=sem1.at[1, me],
            device_id=(chip, core), device_id_type=MESH,
        )
        return copy, jnp.logical_and(chip == s, c == core)

    for i, (dx, j, core) in enumerate(TARGETS):
        cx, row = target(dx, j)
        swap_copy(i).wait_recv()
        b[i] = b[i] + a[c, row, cx, core]
        copy, mine = first_copy(i)

        @pl.when(jnp.logical_not(mine))
        def _():
            copy.start()

        @pl.when(mine)
        def _():
            pltpu.make_async_copy(b.at[i], r1.at[me], sem1.at[1, me]).start()

    row, column = iota((64, 512), 0), iota((64, 512), 1)
    chip = (column // 128) * 32 + 4 * z + (column // 32) % 4
    place = 4 * chip + (column // 8) % 4
    same = row // 8 == column % 8
    lefts = []
    for i in range(2):
        block = (2 * c + i) * 32 + x + 4 * (row // 8)
        left = cos512((4 * block + row % 4) * place + 32 * (row % 8 - row % 4))
        lefts.append(split(jnp.where(same, left, 0.0)))

    frequency = iota((256, 512), 1)
    wide = frequency % 256 + 256 * c
    table_high, table_low = split(cos512(wide * iota((256, 512), 0) - 128 * (frequency // 256)))
    e_high[...] = table_high
    e_low[...] = table_low

    n, source = iota((1024, 256), 1), iota((1024, 256), 0)
    source_block = ((source // 64) % 4) * 32 + source // 256 + 4 * ((source // 8) % 8)
    table_high, table_low = split(cos512(4 * source_block * (n % 128) - 128 * (n // 128)))
    back_high[...] = table_high
    back_low[...] = table_low

    for i in range(16):
        pltpu.make_async_copy(b.at[0], r1.at[i], sem1.at[1, i]).wait()
    parts = []
    for i in range(2):
        right = jnp.concatenate([r1[k, :, 8 * i : 8 * i + 8].reshape(32, 128) for k in range(16)], axis=0)
        right_high, right_low = split(right)
        left_high, left_low = lefts[i]
        both = dot(jnp.concatenate((left_high, left_low), axis=0), right_high)
        parts.append((both[:64] + both[64:]) + dot(left_high, right_low))

    turned = jnp.concatenate(parts, axis=0).T
    for i in range(8):
        zs[i, :8] = parts[0][8 * i : 8 * i + 8]
        zs[i, 8:16] = parts[1][8 * i : 8 * i + 8]
        zs[i, 16:] = turned[16 * i : 16 * i + 16]

    def third_copy(d, h):
        rows = pl.ds(16 * h, 16)
        return pltpu.make_async_remote_copy(
            src_ref=zs.at[(z + d) % 8, rows], dst_ref=r3.at[d, rows],
            send_sem=sem3.at[0, h, d], recv_sem=sem3.at[1, h, d],
            device_id=(z_peer(d), c), device_id_type=MESH,
        )

    def z_sum(h):
        rows = pl.ds(16 * h, 16)
        total = zs[z, rows]
        for d in (1, 7, 2, 6, 3, 5, 4):
            third_copy(d, h).wait_recv()
            total = total + r3[d, rows]
        return total

    for h in (1, 0):
        for d in (4, 3, 5, 2, 6, 1, 7):
            third_copy(d, h).start()

    total = z_sum(1)
    for i in range(4):
        q[i] = total[4 * i : 4 * i + 4]

    def out_copy(dx, core):
        cx = (x + dx) % 4
        copy = pltpu.make_async_remote_copy(
            src_ref=q.at[cx], dst_ref=r5.at[2 * x + c], send_sem=send5.at[dx, core], recv_sem=recv5.at[2 * x + c],
            device_id=(chip_at(y, cx), core), device_id_type=MESH,
        )
        return copy, jnp.logical_and(dx == 0, c == core)

    for dx in (2, 1, 3, 0):
        for core in range(2):
            copy, mine = out_copy(dx, core)

            @pl.when(jnp.logical_not(mine))
            def _():
                copy.start()

            @pl.when(mine)
            def _():
                pltpu.make_async_copy(q.at[x], r5.at[2 * x + c], recv5.at[2 * x + c]).start()

    total = z_sum(0)
    for i in range(2):
        t[i] = total[8 * i : 8 * i + 8]

    def band_copy(j, core):
        row = target(0, j)[1]
        chip = chip_at(2 * c + row, x)
        copy = pltpu.make_async_remote_copy(
            src_ref=t.at[row], dst_ref=r6.at[y], send_sem=send6.at[j, core], recv_sem=recv6.at[y],
            device_id=(chip, core), device_id_type=MESH,
        )
        return copy, jnp.logical_and(chip == s, c == core)

    for j in range(2):
        for core in range(2):
            copy, mine = band_copy(j, core)

            @pl.when(jnp.logical_not(mine))
            def _():
                copy.start()

            @pl.when(mine)
            def _():
                pltpu.make_async_copy(t.at[y % 2], r6.at[y], recv6.at[y]).start()

    lane, rho = iota((8, 256), 1), iota((8, 256), 0)
    angle = (rho % 4) * (lane + 256 * c) + 128 * (rho // 4)
    turn_real, turn_imag = cos512(angle), cos512(angle - 128)
    side = jnp.where(rho < 4, -1.0, 1.0)

    for i in range(8):
        pltpu.make_async_copy(q.at[0], r5.at[i], recv5.at[i]).wait()
    mask = iota((8, 128), 0) == iota((8, 128), 1) % 8
    columns = []
    for j in range(8):
        rows = r5[j]
        columns.append(jnp.concatenate([jnp.where(mask, rows[i : i + 1], 0.0) for i in range(4)], axis=0))
    moved = dot3(jnp.concatenate(columns, axis=1), back_high[...], back_low[...])
    reals, imags = [], []
    for i in range(4):
        tile = moved[8 * i : 8 * i + 8]
        sine = tile[:, 128:]
        pair = tile[:, :128] + side[:, :128] * jnp.concatenate((sine[4:], sine[:4]), axis=0)
        twice = jnp.concatenate((pair, pair), axis=1)
        reals.append(jnp.sum(twice * turn_real, axis=0, keepdims=True))
        imags.append(jnp.sum(twice * turn_imag, axis=0, keepdims=True))
    out[2] = jnp.concatenate(reals, axis=0)
    out[3] = jnp.concatenate(imags, axis=0)

    for i in range(4):
        pltpu.make_async_copy(t.at[0], r6.at[i], recv6.at[i]).wait()
    halves = [jnp.concatenate((r6[2 * i], r6[2 * i + 1]), axis=1) for i in range(2)]
    sums = dot3(jnp.concatenate(halves, axis=0), e_high[...], e_low[...])
    sign = (1 - 2 * (lane % 2)).astype(F32)
    cosine = sums[:8, :256] + sign * sums[8:, :256]
    sine = sums[:8, 256:] + sign * sums[8:, 256:]
    result = cosine - side * jnp.concatenate((sine[4:], sine[:4]), axis=0)
    out[0] = result[:4]
    out[1] = result[4:]

    for i in range(16):
        swap_copy(i).wait_send()
    for d in range(1, 8):
        third_copy(d, 0).wait_send()
        third_copy(d, 1).wait_send()
    copies = [first_copy(i) for i in range(16)]
    copies += [out_copy(dx, core) for dx in range(4) for core in range(2)]
    copies += [band_copy(j, core) for j in range(2) for core in range(2)]
    for copy, mine in copies:

        @pl.when(jnp.logical_not(mine))
        def _():
            copy.wait_send()


def per_device(frames, aperture, upper_pixels, lower_pixels):
    tiled = frames.reshape(128, 4, 4, 128).transpose(0, 2, 1, 3).reshape(128, 2, 8, 128)
    operands = (tiled, aperture.reshape(1, 256), upper_pixels.T, lower_pixels.T)
    hbm = pl.BlockSpec(memory_space=pltpu.HBM)
    dma = pltpu.SemaphoreType.DMA
    both = pl.pallas_call(
        kernel,
        out_shape=pltpu.VMEM((4, 4, 256), F32),
        in_specs=[hbm] * 4,
        out_specs=pl.BlockSpec(memory_space=pltpu.VMEM),
        scratch_shapes=[
            pltpu.VMEM((128, 2, 8, 128), F32),
            pltpu.VMEM((1, 256), jnp.int32),
            pltpu.VMEM((64, 128), jnp.int32),
            pltpu.VMEM((64, 128), jnp.int32),
            pltpu.VMEM((128, 128), F32),
            pltpu.VMEM((2, 2, 4, 2, 4, 16, 128), F32),
            pltpu.VMEM((16, 4, 16, 128), F32),
            pltpu.VMEM((16, 4, 16, 128), F32),
            pltpu.VMEM((8, 32, 128), F32),
            pltpu.VMEM((8, 32, 128), F32),
            pltpu.VMEM((4, 4, 128), F32),
            pltpu.VMEM((8, 4, 128), F32),
            pltpu.VMEM((2, 8, 128), F32),
            pltpu.VMEM((4, 8, 128), F32),
            pltpu.VMEM((256, 512), BF16),
            pltpu.VMEM((256, 512), BF16),
            pltpu.VMEM((1024, 256), BF16),
            pltpu.VMEM((1024, 256), BF16),
            dma((3 + LOADS,)), dma((2, 16)), dma((2, 16)), dma((2, 2, 8)), dma((4, 2)), dma((8,)), dma((2, 2)), dma((4,)),
        ],
        compiler_params=pltpu.CompilerParams(
            collective_id=0, has_side_effects=True, vmem_limit_bytes=32 * 1024 * 1024
        ),
    )(*[pltpu.with_memory_space_constraint(operand, pltpu.HBM) for operand in operands])
    return both[:2], both[2:].transpose(0, 2, 1)


def solution(mesh):
    placed = (P("det", "scan", None), P(), P(), P())
    return jax.shard_map(
        per_device,
        mesh=mesh,
        in_specs=placed,
        out_specs=(P(None, "scan", "det"), P(None, "det", "scan")),
        check_vma=False,
    )
```

time: 33.4 us -> 32.5 us (0.973)
  Pallas kernels: 32.1 us -> 31.2 us
    pallas_call x1, Pallas kernels: 32.1 us -> 31.2 us  [per_device(): pl.pallas_call(kernel, out_shape=pltpu.VMEM((4, 4, 256), F32), in_specs=[...]
where the time goes in v3:
time: 32.5 us; the launch traced here: 32.4 us
  Pallas kernels  31.2 us (96%)
  between operations  0.64 us (2%)
  local copies, waits for them, and re-layouts  0.61 us (2%)
    pallas_call x1, Pallas kernels, per_device(): pl.pallas_call(kernel, out_shape=pltpu.VMEM((4, 4, 256), F32), in_specs=[...  31.2 us

profile of v3, /device:TPU:1, one launch (start us, length us, event | category | flops | bytes accessed | tf_op | source)
XLA Modules:
  0.0 32.4 jit_solution(14402808727746118816)
XLA Ops:
  0.6 31.2 %shard_map.59 = f32[4,4,256]{2,1,0:T(4,128)S(1)} custom-call(f32[128,2,8,128]{3,2,1,0:T(8,128)} %bitcast.10, s32[1,256]{1,0:T(1,128)} %bitcast.13, s32[64,128]{1,0:T(8,128)} %bitcast.11, s32[64,128]{1,0:T(8,128)} %bitcast.12), custom_call_target="tpu_custom_call" | custom-call | tf_op jit(solution)/shard_map/pallas_call | solution.py:337
  31.8 0.6 %slice_bitcast_fusion = (f32[2,256,4]{1,2,0:T(4,128)}, f32[2,4,256]{2,1,0:T(4,128)}) fusion(f32[4,4,256]{2,1,0:T(4,128)S(1)} %shard_map.59), kind=kLoop, calls=%fused_computation | loop fusion | bytes 32768 | tf_op jit(solution)/shard_map/transpose | solution.py:367

commit v4 on v3

--- a/solution.py
+++ b/solution.py
@@ -51,7 +51,7 @@
     frames, aperture, upper, lower,
     out,
     f, ap, up, lo, w, a, b, r1, zs, r3, q, r5, t, r6, e_high, e_low, back_high, back_low,
-    load_sem, swap_sem, sem1, sem3, send5, recv5, send6, recv6,
+    load_sem, swap_sem, sem1, sem3, sem5, sem6,
 ):
     s = lax.axis_index("scan")
     c = lax.axis_index("det")
@@ -132,6 +132,7 @@
     for load in loads[3:]:
         load.wait()
     weighted(1 - c)
+    weighted(c)
 
     pl.semaphore_wait(barrier, jnp.where(home, 22, 30))
 
@@ -141,19 +142,18 @@
         far_row = jnp.where(home, y % 2, 1 - y % 2) * (1 - j) + jnp.where(home, 1 - y % 2, y % 2) * j
         return pltpu.make_async_remote_copy(
             src_ref=a.at[1 - c, far_row, cx, core], dst_ref=b.at[i],
-            send_sem=swap_sem.at[0, i], recv_sem=swap_sem.at[1, i], device_id=(s, 1 - c), device_id_type=MESH,
+            send_sem=swap_sem.at[16], recv_sem=swap_sem.at[i], device_id=(s, 1 - c), device_id_type=MESH,
         )
 
     for i in range(16):
         swap_copy(i).start()
-    weighted(c)
 
     def first_copy(i):
         dx, j, core = TARGETS[i]
         cx, row = target(dx, j)
         chip = chip_at(2 * c + row, cx)
         copy = pltpu.make_async_remote_copy(
-            src_ref=b.at[i], dst_ref=r1.at[me], send_sem=sem1.at[0, i], recv_sem=sem1.at[1, me],
+            src_ref=b.at[i], dst_ref=r1.at[me], send_sem=sem1.at[0], recv_sem=sem1.at[1],
             device_id=(chip, core), device_id_type=MESH,
         )
         return copy, jnp.logical_and(chip == s, c == core)
@@ -163,14 +163,17 @@
         swap_copy(i).wait_recv()
         b[i] = b[i] + a[c, row, cx, core]
         copy, mine = first_copy(i)
-
-        @pl.when(jnp.logical_not(mine))
-        def _():
+        if dx or not j:
             copy.start()
-
-        @pl.when(mine)
-        def _():
-            pltpu.make_async_copy(b.at[i], r1.at[me], sem1.at[1, me]).start()
+        else:
+
+            @pl.when(jnp.logical_not(mine))
+            def _():
+                copy.start()
+
+            @pl.when(mine)
+            def _():
+                pltpu.make_async_copy(b.at[i], r1.at[me], sem1.at[1]).start()
 
     row, column = iota((64, 512), 0), iota((64, 512), 1)
     chip = (column // 128) * 32 + 4 * z + (column // 32) % 4
@@ -194,8 +197,7 @@
     back_high[...] = table_high
     back_low[...] = table_low
 
-    for i in range(16):
-        pltpu.make_async_copy(b.at[0], r1.at[i], sem1.at[1, i]).wait()
+    pltpu.make_async_copy(r1, r1, sem1.at[1]).wait()
     parts = []
     for i in range(2):
         right = jnp.concatenate([r1[k, :, 8 * i : 8 * i + 8].reshape(32, 128) for k in range(16)], axis=0)
@@ -214,7 +216,7 @@
         rows = pl.ds(16 * h, 16)
         return pltpu.make_async_remote_copy(
             src_ref=zs.at[(z + d) % 8, rows], dst_ref=r3.at[d, rows],
-            send_sem=sem3.at[0, h, d], recv_sem=sem3.at[1, h, d],
+            send_sem=sem3.at[h, 0], recv_sem=sem3.at[h, d],
             device_id=(z_peer(d), c), device_id_type=MESH,
         )
 
@@ -230,6 +232,13 @@
         for d in (4, 3, 5, 2, 6, 1, 7):
             third_copy(d, h).start()
 
+    pltpu.make_async_copy(r1, r1, swap_sem.at[16]).wait()
+    pltpu.make_async_copy(r1.at[:15], r1.at[:15], sem1.at[0]).wait()
+
+    @pl.when(jnp.logical_not(home))
+    def _():
+        pltpu.make_async_copy(r1.at[0], r1.at[0], sem1.at[0]).wait()
+
     total = z_sum(1)
     for i in range(4):
         q[i] = total[4 * i : 4 * i + 4]
@@ -237,7 +246,7 @@
     def out_copy(dx, core):
         cx = (x + dx) % 4
         copy = pltpu.make_async_remote_copy(
-            src_ref=q.at[cx], dst_ref=r5.at[2 * x + c], send_sem=send5.at[dx, core], recv_sem=recv5.at[2 * x + c],
+            src_ref=q.at[cx], dst_ref=r5.at[2 * x + c], send_sem=sem5.at[0], recv_sem=sem5.at[1],
             device_id=(chip_at(y, cx), core), device_id_type=MESH,
         )
         return copy, jnp.logical_and(dx == 0, c == core)
@@ -245,14 +254,17 @@
     for dx in (2, 1, 3, 0):
         for core in range(2):
             copy, mine = out_copy(dx, core)
-
-            @pl.when(jnp.logical_not(mine))
-            def _():
+            if dx:
                 copy.start()
-
-            @pl.when(mine)
-            def _():
-                pltpu.make_async_copy(q.at[x], r5.at[2 * x + c], recv5.at[2 * x + c]).start()
+            else:
+
+                @pl.when(jnp.logical_not(mine))
+                def _():
+                    copy.start()
+
+                @pl.when(mine)
+                def _():
+                    pltpu.make_async_copy(q.at[x], r5.at[2 * x + c], sem5.at[1]).start()
 
     total = z_sum(0)
     for i in range(2):
@@ -262,7 +274,7 @@
         row = target(0, j)[1]
         chip = chip_at(2 * c + row, x)
         copy = pltpu.make_async_remote_copy(
-            src_ref=t.at[row], dst_ref=r6.at[y], send_sem=send6.at[j, core], recv_sem=recv6.at[y],
+            src_ref=t.at[row], dst_ref=r6.at[y], send_sem=sem6.at[0], recv_sem=sem6.at[1],
             device_id=(chip, core), device_id_type=MESH,
         )
         return copy, jnp.logical_and(chip == s, c == core)
@@ -270,22 +282,27 @@
     for j in range(2):
         for core in range(2):
             copy, mine = band_copy(j, core)
-
-            @pl.when(jnp.logical_not(mine))
-            def _():
+            if not j:
                 copy.start()
-
-            @pl.when(mine)
-            def _():
-                pltpu.make_async_copy(t.at[y % 2], r6.at[y], recv6.at[y]).start()
-
+            else:
+
+                @pl.when(jnp.logical_not(mine))
+                def _():
+                    copy.start()
+
+                @pl.when(mine)
+                def _():
+                    pltpu.make_async_copy(t.at[y % 2], r6.at[y], sem6.at[1]).start()
+
+    for h in range(2):
+        rows = pl.ds(16 * h, 16)
+        pltpu.make_async_copy(r3.at[1:, rows], r3.at[1:, rows], sem3.at[h, 0]).wait()
     lane, rho = iota((8, 256), 1), iota((8, 256), 0)
     angle = (rho % 4) * (lane + 256 * c) + 128 * (rho // 4)
     turn_real, turn_imag = cos512(angle), cos512(angle - 128)
     side = jnp.where(rho < 4, -1.0, 1.0)
 
-    for i in range(8):
-        pltpu.make_async_copy(q.at[0], r5.at[i], recv5.at[i]).wait()
+    pltpu.make_async_copy(r5, r5, sem5.at[1]).wait()
     mask = iota((8, 128), 0) == iota((8, 128), 1) % 8
     columns = []
     for j in range(8):
@@ -303,8 +320,7 @@
     out[2] = jnp.concatenate(reals, axis=0)
     out[3] = jnp.concatenate(imags, axis=0)
 
-    for i in range(4):
-        pltpu.make_async_copy(t.at[0], r6.at[i], recv6.at[i]).wait()
+    pltpu.make_async_copy(r6, r6, sem6.at[1]).wait()
     halves = [jnp.concatenate((r6[2 * i], r6[2 * i + 1]), axis=1) for i in range(2)]
     sums = dot3(jnp.concatenate(halves, axis=0), e_high[...], e_low[...])
     sign = (1 - 2 * (lane % 2)).astype(F32)
@@ -314,19 +330,12 @@
     out[0] = result[:4]
     out[1] = result[4:]
 
-    for i in range(16):
-        swap_copy(i).wait_send()
-    for d in range(1, 8):
-        third_copy(d, 0).wait_send()
-        third_copy(d, 1).wait_send()
-    copies = [first_copy(i) for i in range(16)]
-    copies += [out_copy(dx, core) for dx in range(4) for core in range(2)]
-    copies += [band_copy(j, core) for j in range(2) for core in range(2)]
-    for copy, mine in copies:
-
-        @pl.when(jnp.logical_not(mine))
-        def _():
-            copy.wait_send()
+    pltpu.make_async_copy(r5.at[:7], r5.at[:7], sem5.at[0]).wait()
+    pltpu.make_async_copy(r6.at[:3], r6.at[:3], sem6.at[0]).wait()
+
+    @pl.when(jnp.logical_not(home))
+    def _():
+        pltpu.make_async_copy(r6.at[0], r6.at[0], sem6.at[0]).wait()
 
 
 def per_device(frames, aperture, upper_pixels, lower_pixels):
@@ -358,7 +367,7 @@
             pltpu.VMEM((256, 512), BF16),
             pltpu.VMEM((1024, 256), BF16),
             pltpu.VMEM((1024, 256), BF16),
-            dma((3 + LOADS,)), dma((2, 16)), dma((2, 16)), dma((2, 2, 8)), dma((4, 2)), dma((8,)), dma((2, 2)), dma((4,)),
+            dma((3 + LOADS,)), dma((17,)), dma((2,)), dma((2, 8)), dma((2,)), dma((2,)),
         ],
         compiler_params=pltpu.CompilerParams(
             collective_id=0, has_side_effects=True, vmem_limit_bytes=32 * 1024 * 1024

time: 32.5 us -> 31.5 us (0.969)
  Pallas kernels: 31.2 us -> 30.2 us
    pallas_call x1, Pallas kernels: 31.2 us -> 30.2 us  [per_device(): pl.pallas_call(kernel, out_shape=pltpu.VMEM((4, 4, 256), F32), in_specs=[...]
where the time goes in v4:
time: 31.5 us; the launch traced here: 31.4 us
  Pallas kernels  30.2 us (96%)
  between operations  0.64 us (2%)
  local copies, waits for them, and re-layouts  0.61 us (2%)
    pallas_call x1, Pallas kernels, per_device(): pl.pallas_call(kernel, out_shape=pltpu.VMEM((4, 4, 256), F32), in_specs=[...  30.2 us

profile of v4, /device:TPU:1, one launch (start us, length us, event | category | flops | bytes accessed | tf_op | source)
XLA Modules:
  0.0 31.4 jit_solution(2447741973668184614)
XLA Ops:
  0.6 30.2 %shard_map.59 = f32[4,4,256]{2,1,0:T(4,128)S(1)} custom-call(f32[128,2,8,128]{3,2,1,0:T(8,128)} %bitcast.10, s32[1,256]{1,0:T(1,128)} %bitcast.13, s32[64,128]{1,0:T(8,128)} %bitcast.11, s32[64,128]{1,0:T(8,128)} %bitcast.12), custom_call_target="tpu_custom_call" | custom-call | tf_op jit(solution)/shard_map/pallas_call | solution.py:346
  30.8 0.6 %slice_bitcast_fusion = (f32[2,256,4]{1,2,0:T(4,128)}, f32[2,4,256]{2,1,0:T(4,128)}) fusion(f32[4,4,256]{2,1,0:T(4,128)S(1)} %shard_map.59), kind=kLoop, calls=%fused_computation | loop fusion | bytes 32768 | tf_op jit(solution)/shard_map/transpose | solution.py:376

commit v5 on v4

--- a/solution.py
+++ b/solution.py
@@ -63,7 +63,7 @@
         return cy * 32 + z * 4 + cx
 
     first_row = jnp.where(home, 1 - y % 2, y % 2)
-    TARGETS = [(dx, j, core) for dx in (2, 1, 3, 0) for j in range(2) for core in range(2)]
+    TARGETS = [(dx, j, k) for k in range(2) for j in range(2) for dx in (2, 1, 3, 0)]
 
     def target(dx, j):
         return (x + dx) % 4, first_row * (1 - j) + (1 - first_row) * j
@@ -137,11 +137,11 @@
     pl.semaphore_wait(barrier, jnp.where(home, 22, 30))
 
     def swap_copy(i):
-        dx, j, core = TARGETS[i]
+        dx, j, k = TARGETS[i]
         cx, row = target(dx, j)
         far_row = jnp.where(home, y % 2, 1 - y % 2) * (1 - j) + jnp.where(home, 1 - y % 2, y % 2) * j
         return pltpu.make_async_remote_copy(
-            src_ref=a.at[1 - c, far_row, cx, core], dst_ref=b.at[i],
+            src_ref=a.at[1 - c, far_row, cx, (1 - c + k) % 2], dst_ref=b.at[i],
             send_sem=swap_sem.at[16], recv_sem=swap_sem.at[i], device_id=(s, 1 - c), device_id_type=MESH,
         )
 
@@ -149,21 +149,21 @@
         swap_copy(i).start()
 
     def first_copy(i):
-        dx, j, core = TARGETS[i]
+        dx, j, k = TARGETS[i]
         cx, row = target(dx, j)
         chip = chip_at(2 * c + row, cx)
         copy = pltpu.make_async_remote_copy(
             src_ref=b.at[i], dst_ref=r1.at[me], send_sem=sem1.at[0], recv_sem=sem1.at[1],
-            device_id=(chip, core), device_id_type=MESH,
-        )
-        return copy, jnp.logical_and(chip == s, c == core)
-
-    for i, (dx, j, core) in enumerate(TARGETS):
+            device_id=(chip, (c + k) % 2), device_id_type=MESH,
+        )
+        return copy, chip == s
+
+    for i, (dx, j, k) in enumerate(TARGETS):
         cx, row = target(dx, j)
         swap_copy(i).wait_recv()
-        b[i] = b[i] + a[c, row, cx, core]
+        b[i] = b[i] + a[c, row, cx, (c + k) % 2]
         copy, mine = first_copy(i)
-        if dx or not j:
+        if dx or not j or k:
             copy.start()
         else:
 

time: 31.5 us -> 30.4 us (0.965)
  Pallas kernels: 30.2 us -> 29.1 us
    pallas_call x1, Pallas kernels: 30.2 us -> 29.1 us  [per_device(): pl.pallas_call(kernel, out_shape=pltpu.VMEM((4, 4, 256), F32), in_specs=[...]
where the time goes in v5:
time: 30.4 us; the launch traced here: 30.3 us
  Pallas kernels  29.1 us (96%)
  between operations  0.64 us (2%)
  local copies, waits for them, and re-layouts  0.61 us (2%)
    pallas_call x1, Pallas kernels, per_device(): pl.pallas_call(kernel, out_shape=pltpu.VMEM((4, 4, 256), F32), in_specs=[...  29.1 us

profile of v5, /device:TPU:1, one launch (start us, length us, event | category | flops | bytes accessed | tf_op | source)
XLA Modules:
  0.0 30.3 jit_solution(11176652729352513253)
XLA Ops:
  0.6 29.1 %shard_map.59 = f32[4,4,256]{2,1,0:T(4,128)S(1)} custom-call(f32[128,2,8,128]{3,2,1,0:T(8,128)} %bitcast.10, s32[1,256]{1,0:T(1,128)} %bitcast.13, s32[64,128]{1,0:T(8,128)} %bitcast.11, s32[64,128]{1,0:T(8,128)} %bitcast.12), custom_call_target="tpu_custom_call" | custom-call | tf_op jit(solution)/shard_map/pallas_call | solution.py:346
  29.7 0.6 %slice_bitcast_fusion = (f32[2,256,4]{1,2,0:T(4,128)}, f32[2,4,256]{2,1,0:T(4,128)}) fusion(f32[4,4,256]{2,1,0:T(4,128)S(1)} %shard_map.59), kind=kLoop, calls=%fused_computation | loop fusion | bytes 32768 | tf_op jit(solution)/shard_map/transpose | solution.py:376

commit v6 on v5

--- a/solution.py
+++ b/solution.py
@@ -163,7 +163,7 @@
         swap_copy(i).wait_recv()
         b[i] = b[i] + a[c, row, cx, (c + k) % 2]
         copy, mine = first_copy(i)
-        if dx or not j or k:
+        if dx or k:
             copy.start()
         else:
 
@@ -212,25 +212,14 @@
         zs[i, 8:16] = parts[1][8 * i : 8 * i + 8]
         zs[i, 16:] = turned[16 * i : 16 * i + 16]
 
-    def third_copy(d, h):
-        rows = pl.ds(16 * h, 16)
+    def third_copy(d):
         return pltpu.make_async_remote_copy(
-            src_ref=zs.at[(z + d) % 8, rows], dst_ref=r3.at[d, rows],
-            send_sem=sem3.at[h, 0], recv_sem=sem3.at[h, d],
+            src_ref=zs.at[(z + d) % 8], dst_ref=r3.at[d], send_sem=sem3.at[0], recv_sem=sem3.at[d],
             device_id=(z_peer(d), c), device_id_type=MESH,
         )
 
-    def z_sum(h):
-        rows = pl.ds(16 * h, 16)
-        total = zs[z, rows]
-        for d in (1, 7, 2, 6, 3, 5, 4):
-            third_copy(d, h).wait_recv()
-            total = total + r3[d, rows]
-        return total
-
-    for h in (1, 0):
-        for d in (4, 3, 5, 2, 6, 1, 7):
-            third_copy(d, h).start()
+    for d in (4, 5, 3, 6, 2, 7, 1):
+        third_copy(d).start()
 
     pltpu.make_async_copy(r1, r1, swap_sem.at[16]).wait()
     pltpu.make_async_copy(r1.at[:15], r1.at[:15], sem1.at[0]).wait()
@@ -239,34 +228,10 @@
     def _():
         pltpu.make_async_copy(r1.at[0], r1.at[0], sem1.at[0]).wait()
 
-    total = z_sum(1)
-    for i in range(4):
-        q[i] = total[4 * i : 4 * i + 4]
-
-    def out_copy(dx, core):
-        cx = (x + dx) % 4
-        copy = pltpu.make_async_remote_copy(
-            src_ref=q.at[cx], dst_ref=r5.at[2 * x + c], send_sem=sem5.at[0], recv_sem=sem5.at[1],
-            device_id=(chip_at(y, cx), core), device_id_type=MESH,
-        )
-        return copy, jnp.logical_and(dx == 0, c == core)
-
-    for dx in (2, 1, 3, 0):
-        for core in range(2):
-            copy, mine = out_copy(dx, core)
-            if dx:
-                copy.start()
-            else:
-
-                @pl.when(jnp.logical_not(mine))
-                def _():
-                    copy.start()
-
-                @pl.when(mine)
-                def _():
-                    pltpu.make_async_copy(q.at[x], r5.at[2 * x + c], sem5.at[1]).start()
-
-    total = z_sum(0)
+    total = zs[z]
+    for d in (1, 7, 2, 6, 3, 5, 4):
+        third_copy(d).wait_recv()
+        total = total + r3[d]
     for i in range(2):
         t[i] = total[8 * i : 8 * i + 8]
 
@@ -280,9 +245,32 @@
         return copy, jnp.logical_and(chip == s, c == core)
 
     for j in range(2):
-        for core in range(2):
+        for core in (1, 0):
             copy, mine = band_copy(j, core)
-            if not j:
+
+            @pl.when(jnp.logical_not(mine))
+            def _():
+                copy.start()
+
+            @pl.when(mine)
+            def _():
+                pltpu.make_async_copy(t.at[y % 2], r6.at[y], sem6.at[1]).start()
+
+    for i in range(4):
+        q[i] = total[16 + 4 * i : 20 + 4 * i]
+
+    def out_copy(dx, core):
+        cx = (x + dx) % 4
+        copy = pltpu.make_async_remote_copy(
+            src_ref=q.at[cx], dst_ref=r5.at[2 * x + c], send_sem=sem5.at[0], recv_sem=sem5.at[1],
+            device_id=(chip_at(y, cx), core), device_id_type=MESH,
+        )
+        return copy, jnp.logical_and(dx == 0, c == core)
+
+    for dx in (2, 1, 3, 0):
+        for core in (1, 0):
+            copy, mine = out_copy(dx, core)
+            if dx:
                 copy.start()
             else:
 
@@ -292,11 +280,9 @@
 
                 @pl.when(mine)
                 def _():
-                    pltpu.make_async_copy(t.at[y % 2], r6.at[y], sem6.at[1]).start()
-
-    for h in range(2):
-        rows = pl.ds(16 * h, 16)
-        pltpu.make_async_copy(r3.at[1:, rows], r3.at[1:, rows], sem3.at[h, 0]).wait()
+                    pltpu.make_async_copy(q.at[x], r5.at[2 * x + c], sem5.at[1]).start()
+
+    pltpu.make_async_copy(r3.at[1:], r3.at[1:], sem3.at[0]).wait()
     lane, rho = iota((8, 256), 1), iota((8, 256), 0)
     angle = (rho % 4) * (lane + 256 * c) + 128 * (rho // 4)
     turn_real, turn_imag = cos512(angle), cos512(angle - 128)
@@ -367,7 +353,7 @@
             pltpu.VMEM((256, 512), BF16),
             pltpu.VMEM((1024, 256), BF16),
             pltpu.VMEM((1024, 256), BF16),
-            dma((3 + LOADS,)), dma((17,)), dma((2,)), dma((2, 8)), dma((2,)), dma((2,)),
+            dma((3 + LOADS,)), dma((17,)), dma((2,)), dma((8,)), dma((2,)), dma((2,)),
         ],
         compiler_params=pltpu.CompilerParams(
             collective_id=0, has_side_effects=True, vmem_limit_bytes=32 * 1024 * 1024

time: 30.4 us -> 30.1 us (level)
  Pallas kernels: 29.1 us -> 28.7 us
    pallas_call x1, Pallas kernels: 29.1 us -> 28.7 us  [per_device(): pl.pallas_call(kernel, out_shape=pltpu.VMEM((4, 4, 256), F32), in_specs=[...]
where the time goes in v6:
time: 30.1 us; the launch traced here: 30 us
  Pallas kernels  28.7 us (95%)
  between operations  0.64 us (2%)
  local copies, waits for them, and re-layouts  0.61 us (2%)
    pallas_call x1, Pallas kernels, per_device(): pl.pallas_call(kernel, out_shape=pltpu.VMEM((4, 4, 256), F32), in_specs=[...  28.7 us
    transpose x1, local copies, waits for them, and re-layouts, per_device(): return (both[:2], both[2:].transpose(0, 2, 1))  0.61 us

profile of v6, /device:TPU:1, one launch (start us, length us, event | category | flops | bytes accessed | tf_op | source)
XLA Modules:
  0.0 30.0 jit_solution(15587240467346568414)
XLA Ops:
  0.6 28.7 %shard_map.59 = f32[4,4,256]{2,1,0:T(4,128)S(1)} custom-call(f32[128,2,8,128]{3,2,1,0:T(8,128)} %bitcast.10, s32[1,256]{1,0:T(1,128)} %bitcast.13, s32[64,128]{1,0:T(8,128)} %bitcast.11, s32[64,128]{1,0:T(8,128)} %bitcast.12), custom_call_target="tpu_custom_call" | custom-call | tf_op jit(solution)/shard_map/pallas_call | solution.py:332
  29.4 0.6 %slice_bitcast_fusion = (f32[2,256,4]{1,2,0:T(4,128)}, f32[2,4,256]{2,1,0:T(4,128)}) fusion(f32[4,4,256]{2,1,0:T(4,128)S(1)} %shard_map.59), kind=kLoop, calls=%fused_computation | loop fusion | bytes 32768 | tf_op jit(solution)/shard_map/transpose | solution.py:362

commit v7 on v6

--- a/solution.py
+++ b/solution.py
@@ -71,6 +71,21 @@
     def z_peer(d):
         return s + ((z + d) % 8 - z) * 4
 
+    barrier = pltpu.get_barrier_semaphore()
+
+    def greet(scan, det):
+        pl.semaphore_signal(barrier, inc=1, device_id=(scan, det), device_id_type=MESH)
+
+    for d in (4, 3, 5, 2, 6, 1, 7):
+        greet(z_peer(d), c)
+    for dx in (2, 1, 3, 0):
+        for dy in (2, 1, 3, 0):
+            if dx or dy:
+                greet(chip_at((y + dy) % 4, (x + dx) % 4), y // 2)
+        if dx:
+            greet(chip_at(y, (x + dx) % 4), 1 - y // 2)
+    greet(s, 1 - c)
+
     loads = [
         pltpu.make_async_copy(upper, up, load_sem.at[0]),
         pltpu.make_async_copy(lower, lo, load_sem.at[1]),
@@ -82,24 +97,6 @@
     for load in loads:
         load.start()
 
-    barrier = pltpu.get_barrier_semaphore()
-
-    def greet(scan, det):
-        pl.semaphore_signal(barrier, inc=1, device_id=(scan, det), device_id_type=MESH)
-
-    for d in (4, 3, 5, 2, 6, 1, 7):
-        greet(z_peer(d), c)
-    for dx in (2, 1, 3, 0):
-        for dy in (2, 1, 3, 0):
-
-            @pl.when(jnp.logical_or(jnp.logical_not(home), dx + dy > 0))
-            def _():
-                greet(chip_at((y + dy) % 4, (x + dx) % 4), y // 2)
-
-        @pl.when(jnp.logical_or(home, dx > 0))
-        def _():
-            greet(chip_at(y, (x + dx) % 4), 1 - y // 2)
-
     for load in loads[:3]:
         load.wait()
     pixel = (iota((128, 128), 0) + 128 * c).astype(F32).astype(BF16)
@@ -141,7 +138,7 @@
         cx, row = target(dx, j)
         far_row = jnp.where(home, y % 2, 1 - y % 2) * (1 - j) + jnp.where(home, 1 - y % 2, y % 2) * j
         return pltpu.make_async_remote_copy(
-            src_ref=a.at[1 - c, far_row, cx, (1 - c + k) % 2], dst_ref=b.at[i],
+            src_ref=a.at[1 - c, far_row, cx, k], dst_ref=b.at[i],
             send_sem=swap_sem.at[16], recv_sem=swap_sem.at[i], device_id=(s, 1 - c), device_id_type=MESH,
         )
 
@@ -154,16 +151,16 @@
         chip = chip_at(2 * c + row, cx)
         copy = pltpu.make_async_remote_copy(
             src_ref=b.at[i], dst_ref=r1.at[me], send_sem=sem1.at[0], recv_sem=sem1.at[1],
-            device_id=(chip, (c + k) % 2), device_id_type=MESH,
-        )
-        return copy, chip == s
+            device_id=(chip, k), device_id_type=MESH,
+        )
+        return copy, jnp.logical_and(chip == s, c == k)
 
     for i, (dx, j, k) in enumerate(TARGETS):
         cx, row = target(dx, j)
         swap_copy(i).wait_recv()
-        b[i] = b[i] + a[c, row, cx, (c + k) % 2]
+        b[i] = b[i] + a[c, row, cx, k]
         copy, mine = first_copy(i)
-        if dx or k:
+        if dx or not j:
             copy.start()
         else:
 
@@ -212,14 +209,24 @@
         zs[i, 8:16] = parts[1][8 * i : 8 * i + 8]
         zs[i, 16:] = turned[16 * i : 16 * i + 16]
 
-    def third_copy(d):
+    def third_copy(d, h):
+        rows = pl.ds(16 * h, 16)
         return pltpu.make_async_remote_copy(
-            src_ref=zs.at[(z + d) % 8], dst_ref=r3.at[d], send_sem=sem3.at[0], recv_sem=sem3.at[d],
+            src_ref=zs.at[(z + d) % 8, rows], dst_ref=r3.at[d, rows], send_sem=sem3.at[0], recv_sem=sem3.at[8 * h + d],
             device_id=(z_peer(d), c), device_id_type=MESH,
         )
 
-    for d in (4, 5, 3, 6, 2, 7, 1):
-        third_copy(d).start()
+    def z_sum(h):
+        rows = pl.ds(16 * h, 16)
+        total = zs[z, rows]
+        for d in (1, 7, 2, 6, 3, 5, 4):
+            third_copy(d, h).wait_recv()
+            total = total + r3[d, rows]
+        return total
+
+    for h in range(2):
+        for d in (4, 5, 3, 6, 2, 7, 1):
+            third_copy(d, h).start()
 
     pltpu.make_async_copy(r1, r1, swap_sem.at[16]).wait()
     pltpu.make_async_copy(r1.at[:15], r1.at[:15], sem1.at[0]).wait()
@@ -228,10 +235,7 @@
     def _():
         pltpu.make_async_copy(r1.at[0], r1.at[0], sem1.at[0]).wait()
 
-    total = zs[z]
-    for d in (1, 7, 2, 6, 3, 5, 4):
-        third_copy(d).wait_recv()
-        total = total + r3[d]
+    total = z_sum(0)
     for i in range(2):
         t[i] = total[8 * i : 8 * i + 8]
 
@@ -247,17 +251,21 @@
     for j in range(2):
         for core in (1, 0):
             copy, mine = band_copy(j, core)
-
-            @pl.when(jnp.logical_not(mine))
-            def _():
+            if not j:
                 copy.start()
-
-            @pl.when(mine)
-            def _():
-                pltpu.make_async_copy(t.at[y % 2], r6.at[y], sem6.at[1]).start()
-
+            else:
+
+                @pl.when(jnp.logical_not(mine))
+                def _():
+                    copy.start()
+
+                @pl.when(mine)
+                def _():
+                    pltpu.make_async_copy(t.at[y % 2], r6.at[y], sem6.at[1]).start()
+
+    total = z_sum(1)
     for i in range(4):
-        q[i] = total[16 + 4 * i : 20 + 4 * i]
+        q[i] = total[4 * i : 4 * i + 4]
 
     def out_copy(dx, core):
         cx = (x + dx) % 4
@@ -287,6 +295,16 @@
     angle = (rho % 4) * (lane + 256 * c) + 128 * (rho // 4)
     turn_real, turn_imag = cos512(angle), cos512(angle - 128)
     side = jnp.where(rho < 4, -1.0, 1.0)
+
+    pltpu.make_async_copy(r6, r6, sem6.at[1]).wait()
+    halves = [jnp.concatenate((r6[2 * i], r6[2 * i + 1]), axis=1) for i in range(2)]
+    sums = dot3(jnp.concatenate(halves, axis=0), e_high[...], e_low[...])
+    sign = (1 - 2 * (lane % 2)).astype(F32)
+    cosine = sums[:8, :256] + sign * sums[8:, :256]
+    sine = sums[:8, 256:] + sign * sums[8:, 256:]
+    result = cosine - side * jnp.concatenate((sine[4:], sine[:4]), axis=0)
+    out[0] = result[:4]
+    out[1] = result[4:]
 
     pltpu.make_async_copy(r5, r5, sem5.at[1]).wait()
     mask = iota((8, 128), 0) == iota((8, 128), 1) % 8
@@ -305,16 +323,6 @@
         imags.append(jnp.sum(twice * turn_imag, axis=0, keepdims=True))
     out[2] = jnp.concatenate(reals, axis=0)
     out[3] = jnp.concatenate(imags, axis=0)
-
-    pltpu.make_async_copy(r6, r6, sem6.at[1]).wait()
-    halves = [jnp.concatenate((r6[2 * i], r6[2 * i + 1]), axis=1) for i in range(2)]
-    sums = dot3(jnp.concatenate(halves, axis=0), e_high[...], e_low[...])
-    sign = (1 - 2 * (lane % 2)).astype(F32)
-    cosine = sums[:8, :256] + sign * sums[8:, :256]
-    sine = sums[:8, 256:] + sign * sums[8:, 256:]
-    result = cosine - side * jnp.concatenate((sine[4:], sine[:4]), axis=0)
-    out[0] = result[:4]
-    out[1] = result[4:]
 
     pltpu.make_async_copy(r5.at[:7], r5.at[:7], sem5.at[0]).wait()
     pltpu.make_async_copy(r6.at[:3], r6.at[:3], sem6.at[0]).wait()
@@ -353,7 +361,7 @@
             pltpu.VMEM((256, 512), BF16),
             pltpu.VMEM((1024, 256), BF16),
             pltpu.VMEM((1024, 256), BF16),
-            dma((3 + LOADS,)), dma((17,)), dma((2,)), dma((8,)), dma((2,)), dma((2,)),
+            dma((3 + LOADS,)), dma((17,)), dma((2,)), dma((16,)), dma((2,)), dma((2,)),
         ],
         compiler_params=pltpu.CompilerParams(
             collective_id=0, has_side_effects=True, vmem_limit_bytes=32 * 1024 * 1024

time: 30.1 us -> 30.1 us (level)
  no operation moved by 1% of the time
where the time goes in v7:
time: 30.1 us; the launch traced here: 30 us
  Pallas kernels  28.7 us (95%)
  between operations  0.64 us (2%)
  local copies, waits for them, and re-layouts  0.61 us (2%)
    pallas_call x1, Pallas kernels, per_device(): pl.pallas_call(kernel, out_shape=pltpu.VMEM((4, 4, 256), F32), in_specs=[...  28.7 us
    transpose x1, local copies, waits for them, and re-layouts, per_device(): return (both[:2], both[2:].transpose(0, 2, 1))  0.61 us

profile of v7, /device:TPU:1, one launch (start us, length us, event | category | flops | bytes accessed | tf_op | source)
XLA Modules:
  0.0 30.0 jit_solution(39450404920967949)
XLA Ops:
  0.6 28.7 %shard_map.59 = f32[4,4,256]{2,1,0:T(4,128)S(1)} custom-call(f32[128,2,8,128]{3,2,1,0:T(8,128)} %bitcast.10, s32[1,256]{1,0:T(1,128)} %bitcast.13, s32[64,128]{1,0:T(8,128)} %bitcast.11, s32[64,128]{1,0:T(8,128)} %bitcast.12), custom_call_target="tpu_custom_call" | custom-call | tf_op jit(solution)/shard_map/pallas_call | solution.py:340
  29.4 0.6 %slice_bitcast_fusion = (f32[2,256,4]{1,2,0:T(4,128)}, f32[2,4,256]{2,1,0:T(4,128)}) fusion(f32[4,4,256]{2,1,0:T(4,128)S(1)} %shard_map.59), kind=kLoop, calls=%fused_computation | loop fusion | bytes 32768 | tf_op jit(solution)/shard_map/transpose | solution.py:370

commit v8 on v6

--- a/solution.py
+++ b/solution.py
@@ -71,6 +71,21 @@
     def z_peer(d):
         return s + ((z + d) % 8 - z) * 4
 
+    barrier = pltpu.get_barrier_semaphore()
+
+    def greet(scan, det):
+        pl.semaphore_signal(barrier, inc=1, device_id=(scan, det), device_id_type=MESH)
+
+    for d in (4, 3, 5, 2, 6, 1, 7):
+        greet(z_peer(d), c)
+    for dx in (2, 1, 3, 0):
+        for dy in (2, 1, 3, 0):
+            if dx or dy:
+                greet(chip_at((y + dy) % 4, (x + dx) % 4), y // 2)
+        if dx:
+            greet(chip_at(y, (x + dx) % 4), 1 - y // 2)
+    greet(s, 1 - c)
+
     loads = [
         pltpu.make_async_copy(upper, up, load_sem.at[0]),
         pltpu.make_async_copy(lower, lo, load_sem.at[1]),
@@ -82,24 +97,6 @@
     for load in loads:
         load.start()
 
-    barrier = pltpu.get_barrier_semaphore()
-
-    def greet(scan, det):
-        pl.semaphore_signal(barrier, inc=1, device_id=(scan, det), device_id_type=MESH)
-
-    for d in (4, 3, 5, 2, 6, 1, 7):
-        greet(z_peer(d), c)
-    for dx in (2, 1, 3, 0):
-        for dy in (2, 1, 3, 0):
-
-            @pl.when(jnp.logical_or(jnp.logical_not(home), dx + dy > 0))
-            def _():
-                greet(chip_at((y + dy) % 4, (x + dx) % 4), y // 2)
-
-        @pl.when(jnp.logical_or(home, dx > 0))
-        def _():
-            greet(chip_at(y, (x + dx) % 4), 1 - y // 2)
-
     for load in loads[:3]:
         load.wait()
     pixel = (iota((128, 128), 0) + 128 * c).astype(F32).astype(BF16)
@@ -244,8 +241,8 @@
         )
         return copy, jnp.logical_and(chip == s, c == core)
 
-    for j in range(2):
-        for core in (1, 0):
+    for core in (1, 0):
+        for j in range(2):
             copy, mine = band_copy(j, core)
 
             @pl.when(jnp.logical_not(mine))

time: 30.1 us -> 30.1 us (level)
  no operation moved by 1% of the time
where the time goes in v8:
time: 30.1 us; the launch traced here: 30 us
  Pallas kernels  28.7 us (95%)
  between operations  0.64 us (2%)
  local copies, waits for them, and re-layouts  0.61 us (2%)
    pallas_call x1, Pallas kernels, per_device(): pl.pallas_call(kernel, out_shape=pltpu.VMEM((4, 4, 256), F32), in_specs=[...  28.7 us
    transpose x1, local copies, waits for them, and re-layouts, per_device(): return (both[:2], both[2:].transpose(0, 2, 1))  0.61 us

profile of v8, /device:TPU:1, one launch (start us, length us, event | category | flops | bytes accessed | tf_op | source)
XLA Modules:
  0.0 30.0 jit_solution(15393686665401868638)
XLA Ops:
  0.6 28.7 %shard_map.59 = f32[4,4,256]{2,1,0:T(4,128)S(1)} custom-call(f32[128,2,8,128]{3,2,1,0:T(8,128)} %bitcast.10, s32[1,256]{1,0:T(1,128)} %bitcast.13, s32[64,128]{1,0:T(8,128)} %bitcast.11, s32[64,128]{1,0:T(8,128)} %bitcast.12), custom_call_target="tpu_custom_call" | custom-call | tf_op jit(solution)/shard_map/pallas_call | solution.py:329
  29.4 0.6 %slice_bitcast_fusion = (f32[2,256,4]{1,2,0:T(4,128)}, f32[2,4,256]{2,1,0:T(4,128)}) fusion(f32[4,4,256]{2,1,0:T(4,128)S(1)} %shard_map.59), kind=kLoop, calls=%fused_computation | loop fusion | bytes 32768 | tf_op jit(solution)/shard_map/transpose | solution.py:359
